TPU v7x, 32 devices: a whole 2x2x4 slice. The times are simulated.
32 devices in a mesh: dp: 8 (over z, x), seq: 4 (over y, core).
Axes of the slice: x: 2, y: 2, z: 4, core: 2. Of those that a mesh axis runs over, the one named last changes fastest.
Arguments:
- block_input: bfloat16 [8, 1024, 1024], P('dp', 'seq'), may hold values from -6 to 6
- output_grad: bfloat16 [8, 1024, 1024], P('dp', 'seq'), may hold values from -9 to 9
- row_lengths: int32 [8], P('dp'), may hold values from 341 to 1024, as said below
- qkv_weight: float32 [2, 1024, 3, 1024], P(None, 'dp', None, 'seq'), may hold values from -0.1875 to 0.1875
- proj_weight: float32 [2, 1024, 1024], P(None, 'seq', 'dp'), may hold values from -0.5 to 0.5
- up_weight: float32 [2, 1024, 4096], P(None, 'dp', 'seq'), may hold values from -0.1875 to 0.1875
- down_weight: float32 [2, 4096, 1024], P(None, 'seq', 'dp'), may hold values from -0.125 to 0.125
- norm_params: float32 [2, 4, 1024], P(None, None, ('dp', 'seq')), may hold values from -2 to 2
- qkv_first: float32 [2, 1024, 3, 1024], P(None, 'dp', None, 'seq'), may hold values from -0.00012207031 to 0.00012207031
- proj_first: float32 [2, 1024, 1024], P(None, 'seq', 'dp'), may hold values from -0.00012207031 to 0.00012207031
- up_first: float32 [2, 1024, 4096], P(None, 'dp', 'seq'), may hold values from -0.00012207031 to 0.00012207031
- down_first: float32 [2, 4096, 1024], P(None, 'seq', 'dp'), may hold values from -0.00012207031 to 0.00012207031
- norm_first: float32 [2, 4, 1024], P(None, None, ('dp', 'seq')), may hold values from -0.00012207031 to 0.00012207031
- qkv_second: float32 [2, 1024, 3, 1024], P(None, 'dp', None, 'seq'), may hold values from 1.3113022e-10 to 5.1657356e-10
- proj_second: float32 [2, 1024, 1024], P(None, 'seq', 'dp'), may hold values from 1.3113022e-10 to 5.1657356e-10
- up_second: float32 [2, 1024, 4096], P(None, 'dp', 'seq'), may hold values from 1.3113022e-10 to 5.1657356e-10
- down_second: float32 [2, 4096, 1024], P(None, 'seq', 'dp'), may hold values from 1.3113022e-10 to 5.1657356e-10
- norm_second: float32 [2, 4, 1024], P(None, None, ('dp', 'seq')), may hold values from 1.3113022e-10 to 5.1657356e-10
Outputs:
- block_output: float32 [8, 1024, 1024], P('dp', 'seq')
- input_grad: float32 [8, 1024, 1024], P('dp', 'seq')
- grad_norm: float32 [], replicated
- qkv_grad: float32 [2, 1024, 3, 1024], P(None, 'dp', None, 'seq')
- proj_grad: float32 [2, 1024, 1024], P(None, 'seq', 'dp')
- up_grad: float32 [2, 1024, 4096], P(None, 'dp', 'seq')
- down_grad: float32 [2, 4096, 1024], P(None, 'seq', 'dp')
- norm_grad: float32 [2, 4, 1024], P(None, None, ('dp', 'seq'))
- qkv_momentum: float32 [2, 1024, 3, 1024], P(None, 'dp', None, 'seq')
- proj_momentum: float32 [2, 1024, 1024], P(None, 'seq', 'dp')
- up_momentum: float32 [2, 1024, 4096], P(None, 'dp', 'seq')
- down_momentum: float32 [2, 4096, 1024], P(None, 'seq', 'dp')
- norm_momentum: float32 [2, 4, 1024], P(None, None, ('dp', 'seq'))
- qkv_variance: float32 [2, 1024, 3, 1024], P(None, 'dp', None, 'seq')
- proj_variance: float32 [2, 1024, 1024], P(None, 'seq', 'dp')
- up_variance: float32 [2, 1024, 4096], P(None, 'dp', 'seq')
- down_variance: float32 [2, 4096, 1024], P(None, 'seq', 'dp')
- norm_variance: float32 [2, 4, 1024], P(None, None, ('dp', 'seq'))
- qkv_new: float32 [2, 1024, 3, 1024], P(None, 'dp', None, 'seq')
- proj_new: float32 [2, 1024, 1024], P(None, 'seq', 'dp')
- up_new: float32 [2, 1024, 4096], P(None, 'dp', 'seq')
- down_new: float32 [2, 4096, 1024], P(None, 'seq', 'dp')
- norm_new: float32 [2, 4, 1024], P(None, None, ('dp', 'seq'))
- qkv_copy: bfloat16 [2, 1024, 3, 1024], P(None, 'dp', None, 'seq')
- proj_copy: bfloat16 [2, 1024, 1024], P(None, 'seq', 'dp')
- up_copy: bfloat16 [2, 1024, 4096], P(None, 'dp', 'seq')
- down_copy: bfloat16 [2, 4096, 1024], P(None, 'seq', 'dp')
- norm_copy: bfloat16 [2, 4, 1024], P(None, None, ('dp', 'seq'))
Inputs may be any that keep to these rules, and one draw needn't show every extreme that they name: Slots of row r below row_lengths[r] hold real tokens, the others padding. In every draw one row is 1024 long and one row is 341 long.
All inputs are finite; a program needn't handle non-finite values.
Results may differ from a plain program's by a relative error of at most 0.025.
Values may be sent and summed in bfloat16 or wider, within the bound.
A program may use at most 320 MiB of HBM per device.

v0:
```python
import functools

import jax
import jax.numpy as jnp
import numpy as np
from jax import lax
from jax.experimental import pallas as pl
from jax.experimental.pallas import tpu as pltpu
from jax.sharding import PartitionSpec as P

H = 8
HD = 128
STEP = 5
CORES = 2
ZSIZE = 4

EPS_NORM = 1e-05
BETA_ONE = 0.5
BETA_TWO = 0.75
LEARN_RATE = 0.03
NORM_RATE = 0.3
WEIGHT_DECAY = 0.1
CLIP_NORM = 0.1
ADAM_EPS = 1e-08

UNITS = 12
DEPTH = 2
PUMPS = (
    ((0, 1, 2), (15, 16)),
    ((3,), (17,)),
    ((4,), ()),
    ((5, 6), (18, 19)),
    ((7,), (20, 21)),
    ((8,), ()),
    ((9,), (22,)),
    ((10, 11), (23,)),
    ((12, 13, 14), ()),
)

F32 = jnp.float32
BF16 = jnp.bfloat16
MESH = pl.DeviceIdType.MESH
SCORE_SCALE = HD ** (-0.5)
GELU_A = (2.0 / np.pi) ** 0.5
GELU_B = 0.044715


def slope_table(head_count):
    return np.power(2.0, -8.0 * (np.arange(head_count) + 1.0) / head_count)


def slope_at(head):
    value = jnp.float32(0.0)
    for index, slope in enumerate(slope_table(H)):
        value = jnp.where(head == index, jnp.float32(slope), value)
    return value


def weight_cols(c):
    return pl.ds(0, 3 * c), pl.ds(3 * c, c), pl.ds(4 * c, 4 * c), pl.ds(8 * c, 4 * c)


def mm_nn(a, b):
    return lax.dot_general(a, b, (((1,), (0,)), ((), ())), preferred_element_type=F32)


def mm_nt(a, b):
    return lax.dot_general(a, b, (((1,), (1,)), ((), ())), preferred_element_type=F32)


def mm_tn(a, b):
    return lax.dot_general(a, b, (((0,), (0,)), ((), ())), preferred_element_type=F32)


def normalise(v):
    centered = v - jnp.mean(v, axis=-1, keepdims=True)
    inverse = lax.rsqrt(jnp.mean(centered * centered, axis=-1, keepdims=True) + EPS_NORM)
    return centered * inverse, inverse


def rows_of(index, size):
    return pl.ds(pl.multiple_of(index * size, size), size)


class Place:
    def __init__(self, zn, xn, yn):
        self.zn, self.xn, self.yn = zn, xn, yn
        self.dp = lax.axis_index("dp")
        self.seq = lax.axis_index("seq")
        self.z, self.x = self.dp // xn, lax.rem(self.dp, xn)
        self.y, self.c = self.seq // CORES, lax.rem(self.seq, CORES)

    def zo(self, k):
        return lax.rem(self.z + k + self.zn, self.zn)

    def xo(self, k):
        return lax.rem(self.x + k + self.xn, self.xn)

    def yo(self, k):
        return lax.rem(self.y + k + self.yn, self.yn)

    def dev(self, dz=0, dx=0, dy=0, dc=0):
        core = (1 - self.c) if dc else self.c
        return (self.zo(dz) * self.xn + self.xo(dx), self.yo(dy) * CORES + core)

    def dp_at(self, dz, dx):
        return self.zo(dz) * self.xn + self.xo(dx)

    def seq_at(self, dy, dc):
        core = (1 - self.c) if dc else self.c
        return self.yo(dy) * CORES + core

    def peers(self):
        out = [self.dev(dc=1)]
        out += [self.dev(dy=k) for k in range(1, self.yn)]
        out += [self.dev(dx=k) for k in range(1, self.xn)]
        out += [self.dev(dz=k) for k in range(1, self.zn)]
        return out

    def barrier(self):
        sem = pltpu.get_barrier_semaphore()
        peers = self.peers()
        for peer in peers:
            pl.semaphore_signal(sem, inc=1, device_id=peer, device_id_type=MESH)
        pl.semaphore_wait(sem, len(peers))


def near_first(count):
    order = []
    for k in range(1, count):
        order.append((min(k, count - k), k))
    return [k for unused, k in sorted(order)]


def remote(src, dst, send, recv, dev):
    return pltpu.make_async_remote_copy(
        src_ref=src, dst_ref=dst, send_sem=send, recv_sem=recv, device_id=dev, device_id_type=MESH
    )


def all_sum(place, value, slots, send, recv):
    stages = (
        (CORES, place.c, lambda k: place.dev(dc=1), lambda k: 1 - place.c),
        (place.yn, place.y, lambda k: place.dev(dy=k), lambda k: place.yo(-k)),
        (place.xn, place.x, lambda k: place.dev(dx=k), lambda k: place.xo(-k)),
        (place.zn, place.z, lambda k: place.dev(dz=k), lambda k: place.zo(-k)),
    )
    base = 0
    at = 0
    for size, mine, target, origin in stages:
        slots[base + mine] = value
        own = slots.at[base + mine]
        for k in range(1, size):
            remote(own, own, send.at[at + k - 1], recv.at[at + k - 1], target(k)).start()
        for k in range(1, size):
            came = slots.at[base + origin(k)]
            remote(came, came, send.at[at + k - 1], recv.at[at + k - 1], target(k)).wait_recv()
        for k in range(1, size):
            remote(own, own, send.at[at + k - 1], recv.at[at + k - 1], target(k)).wait_send()
        value = slots[base]
        for k in range(1, size):
            value = value + slots[base + k]
        base += size
        at += size - 1
    return value


def sum_slots(zn, xn, yn):
    return CORES + yn + xn + zn, 1 + (yn - 1) + (xn - 1) + (zn - 1)


class Gather:
    def __init__(self, place, buf, block, send, recv):
        self.p, self.buf, self.block, self.send, self.recv = place, buf, block, send, recv

    def at(self, dy, dc):
        return self.buf.at[rows_of(self.p.seq_at(dy, dc), self.block)]

    def start(self):
        p, own = self.p, self.at(0, 0)
        for k in range(1, p.yn):
            remote(own, own, self.send.at[k], self.recv.at[k], p.dev(dy=k)).start()
        remote(own, own, self.send.at[0], self.recv.at[0], p.dev(dc=1)).start()

    def wait_chip(self):
        came = self.at(0, 1)
        remote(came, came, self.send.at[0], self.recv.at[0], self.p.dev(dc=1)).wait_recv()

    def forward(self):
        p = self.p
        for k in range(1, p.yn):
            came = self.at(-k, 0)
            remote(came, came, self.send.at[k], self.recv.at[k], p.dev(dy=k)).wait_recv()
            f = p.yn - 1 + k
            remote(came, came, self.send.at[f], self.recv.at[f], p.dev(dc=1)).start()

    def wait_rest(self):
        p = self.p
        for k in range(1, p.yn):
            f = p.yn - 1 + k
            came = self.at(-k, 1)
            remote(came, came, self.send.at[f], self.recv.at[f], p.dev(dc=1)).wait_recv()
        own = self.at(0, 0)
        for k in range(1, p.yn):
            remote(own, own, self.send.at[k], self.recv.at[k], p.dev(dy=k)).wait_send()
            f = p.yn - 1 + k
            sent = self.at(-k, 0)
            remote(sent, sent, self.send.at[f], self.recv.at[f], p.dev(dc=1)).wait_send()
        remote(own, own, self.send.at[0], self.recv.at[0], p.dev(dc=1)).wait_send()


class Scatter:
    def __init__(self, place, sbuf, rbuf, ysend, yrecv, acc, send, recv):
        self.p = place
        self.sbuf, self.rbuf, self.ysend, self.yrecv, self.acc = sbuf, rbuf, ysend, yrecv, acc
        self.send, self.recv = send, recv

    def core(self, k):
        return remote(
            self.sbuf.at[k], self.rbuf.at[k], self.send.at[k], self.recv.at[k], self.p.dev(dc=1)
        )

    def cross(self, k):
        s = self.p.yn + k - 1
        return remote(
            self.ysend.at[k - 1],
            self.yrecv.at[k - 1],
            self.send.at[s],
            self.recv.at[s],
            self.p.dev(dy=k),
        )

    def start(self, part):
        p = self.p
        for k in list(range(1, p.yn)) + [0]:
            self.sbuf[k] = part(p.seq_at(k, 1)).astype(BF16)
            self.core(k).start()
            mine = part(p.seq_at(k, 0))
            self.core(k).wait_recv()
            mine = mine + self.rbuf[k].astype(F32)
            if k:
                self.ysend[k - 1] = mine.astype(BF16)
                self.cross(k).start()
            else:
                self.acc[...] = mine

    def wait(self):
        p = self.p
        for k in range(1, p.yn):
            self.cross(k).wait_recv()
        for k in range(1, p.yn):
            self.cross(k).wait_send()
        for k in range(p.yn):
            self.core(k).wait_send()

    def rows(self, at):
        value = self.acc[at, :]
        for k in range(1, self.p.yn):
            value = value + self.yrecv[k - 1, at, :].astype(F32)
        return value


def row_loop(total, step, fn):
    def one(i, unused):
        fn(rows_of(i, step))
        return unused

    lax.fori_loop(0, total // step, one, 0)


def forward_kernel(dims, *refs):
    (layers, slots, width, block, local_width, local_ff, groups, zn, xn, yn) = dims
    heads = local_width // HD
    shard = width // groups
    refs = list(refs)

    def take(count):
        out = refs[:count]
        del refs[:count]
        return out

    lengths, x_in, norm_in = take(3)
    masters = take(4)
    out, norm_out = take(2)
    w_save = take(1)[0]
    xn1_save, xn2_save, qkv_save, ctx_save, lse_save, act_save, dact_save, hid_save, mid_save = take(9)
    w = take(1)[0]
    xn1, xn2, qkv, ctx, lse, act, dact, hid, mid, upper, ws, norm_place = take(12)
    sbuf, rbuf, ysend, yrecv, acc, nslots = take(6)
    zsend, zrecv, xsend, xrecv, own_sem, wsave_sem = take(6)
    ag_send, ag_recv, rs_send, rs_recv, ns_send, ns_recv, save_sem = take(7)

    p = Place(zn, xn, yn)
    z_order = near_first(zn)
    length = lengths[0]
    cols_qkv, cols_o, cols_up, cols_down = weight_cols(local_width)

    unit_count = UNITS * layers
    slopes = [slope_at(p.seq * heads + h) for h in range(heads)]

    def shard_rows(index):
        return rows_of(index, shard)

    def unit_cols(u):
        return pl.ds((u % UNITS) * local_width, local_width)

    def z_copy(u, dz, origin):
        l, cols = u // UNITS, unit_cols(u)
        return remote(
            ws.at[l, :, cols],
            w.at[l, shard_rows(origin), cols],
            zsend.at[u, dz - 1],
            zrecv.at[u, dz - 1],
            p.dev(dz=dz),
        )

    def x_copy(u, dx, dz, origin):
        l, cols = u // UNITS, unit_cols(u)
        there = w.at[l, shard_rows(origin), cols]
        return remote(
            there if dz else ws.at[l, :, cols],
            there,
            xsend.at[u, dx - 1, dz],
            xrecv.at[u, dx - 1, dz],
            p.dev(dx=dx),
        )

    def own_copy(l):
        return pltpu.make_async_copy(ws.at[l], w.at[l, shard_rows(p.dp)], own_sem.at[l])

    def prepare(u):
        l, v = divmod(u, UNITS)
        cols = unit_cols(u)
        if v < 3:
            ws[l, :, cols] = masters[0][l, v].astype(BF16)
        elif 4 <= v < 8:
            ws[l, :, cols] = masters[2][l, :, pl.ds((v - 4) * local_width, local_width)].astype(BF16)
        else:
            source, base = (masters[1], 0) if v == 3 else (masters[3], (v - 8) * local_width)
            for c in range(local_width // 128):
                turned = source[l, pl.ds(base + c * 128, 128), :].T
                ws[l, :, pl.ds((v % UNITS) * local_width + c * 128, 128)] = turned.astype(BF16)

    def start_unit(u):
        for dz in z_order:
            z_copy(u, dz, p.dp).start()
        for dx in range(1, xn):
            x_copy(u, dx, 0, p.dp).start()

    def pump(u):
        for dz in z_order:
            z_copy(u, dz, p.dp_at(-dz, 0)).wait_recv()
            for dx in range(1, xn):
                x_copy(u, dx, dz, p.dp_at(-dz, 0)).start()
        if u + DEPTH < unit_count:
            start_unit(u + DEPTH)

    def pumps(l, *tables):
        for at, units in enumerate(tables):
            if units:

                @pl.when(l == at)
                def _(units=units):
                    for u in units:
                        pump(u)

    def save_weight(l):
        return pltpu.make_async_copy(w.at[l], w_save.at[l], wsave_sem.at[l])

    def need(l, low, high):
        def one(v, unused):
            u = UNITS * l + v
            for dz in range(zn):
                for dx in range(1, xn):
                    at = w.at[0, shard_rows(p.dp_at(-dz, -dx)), pl.ds(0, local_width)]
                    remote(
                        at, at, xsend.at[u, dx - 1, dz], xrecv.at[u, dx - 1, dz], p.dev(dx=dx)
                    ).wait_recv()
            return unused

        lax.fori_loop(low, high, one, 0)

    def finish_weight(l):
        def one(v, unused):
            u = UNITS * l + v
            at = ws.at[0, :, pl.ds(0, local_width)]
            for dz in z_order:
                remote(
                    at, at, zsend.at[u, dz - 1], zrecv.at[u, dz - 1], p.dev(dz=dz)
                ).wait_send()
            for dz in range(zn):
                for dx in range(1, xn):
                    remote(
                        at, at, xsend.at[u, dx - 1, dz], xrecv.at[u, dx - 1, dz], p.dev(dx=dx)
                    ).wait_send()
            return unused

        lax.fori_loop(0, UNITS, one, 0)
        save_weight(l).wait()

    def save(l, which, src, dst):
        return pltpu.make_async_copy(src, dst, save_sem.at[l, which])

    def saves(l):
        return (
            save(l, 0, xn1.at[l], xn1_save.at[l]),
            save(l, 1, xn2.at[l], xn2_save.at[l]),
            save(l, 2, qkv.at[l], qkv_save.at[l]),
            save(l, 3, ctx.at[l], ctx_save.at[l]),
            save(l, 4, lse.at[l], lse_save.at[l]),
            save(l, 5, act.at[l], act_save.at[l]),
            save(l, 6, dact.at[l], dact_save.at[l]),
            save(l, 7, hid.at[l], hid_save.at[l]),
            save(l, 8, mid.at[l], mid_save.at[l]),
        )

    p.barrier()
    for u in range(DEPTH):
        prepare(u)
        start_unit(u)
    piece = width // (groups * CORES * yn)
    at_lane = (p.dp * CORES * yn + p.seq) * piece
    norm_place[...] = jnp.zeros_like(norm_place)
    norm_place[:, rows_of(at_lane // 128, 128)] = pltpu.roll(norm_in[...], lax.rem(at_lane, 128), 1)
    norm_out[...] = all_sum(p, norm_place[...], nslots, ns_send, ns_recv)
    for u in range(DEPTH, UNITS):
        prepare(u)
    own_copy(0).start()

    def load_in(at):
        hid[0, at, :] = x_in[at, :].astype(F32)

    row_loop(block, 64, load_in)
    first = p.seq * block

    def norm_row(index):
        return norm_out[pl.ds(index, 1), :]

    def norm_into(l, source, target, row):
        gain, bias = norm_row(4 * l + row), norm_row(4 * l + row + 1)

        def one(i, unused):
            scaled, inverse = normalise(source[l, rows_of(i, 32), :])
            at = pl.ds(pl.multiple_of(first + i * 32, 32), 32)
            target[l, at, :] = (scaled * gain + bias).astype(BF16)
            return unused

        lax.fori_loop(0, block // 32, one, 0)

    def attention(l):
        key_at = lax.broadcasted_iota(jnp.int32, (1, slots), 1)
        step = 256
        causal = lax.broadcasted_iota(jnp.int32, (step, step), 1) <= lax.broadcasted_iota(
            jnp.int32, (step, step), 0
        )
        for h in range(heads):
            bias = jnp.where(key_at < length, slopes[h] * key_at.astype(F32), -jnp.inf)
            cols = pl.ds(h * HD, HD)
            for b in range(slots // step):
                here = pl.ds(b * step, step)
                before = pl.ds(0, b * step)
                k_cols = pl.ds(local_width + h * HD, HD)
                v_cols = pl.ds(2 * local_width + h * HD, HD)
                q = qkv[l, here, cols]
                raw = mm_nt(q, qkv[l, here, k_cols]) * SCORE_SCALE + bias[:, b * step : (b + 1) * step]
                raw = jnp.where(causal, raw, -jnp.inf)
                top = jnp.max(raw, axis=1, keepdims=True)
                if b:
                    past = mm_nt(q, qkv[l, before, k_cols]) * SCORE_SCALE + bias[:, : b * step]
                    top = jnp.maximum(top, jnp.max(past, axis=1, keepdims=True))
                e_here = jnp.exp(raw - top)
                total = jnp.sum(e_here, axis=1, keepdims=True)
                value = mm_nn(e_here.astype(BF16), qkv[l, here, v_cols])
                if b:
                    e_past = jnp.exp(past - top)
                    total = total + jnp.sum(e_past, axis=1, keepdims=True)
                    value = value + mm_nn(e_past.astype(BF16), qkv[l, before, v_cols])
                ctx[l, here, cols] = (value / total).astype(BF16)
                lse[l, here, pl.ds(h, 1)] = top + jnp.log(total)

    def layer(l, unused):
        last = layers - 1
        g_one = Gather(p, xn1.at[l], block, ag_send.at[2 * l], ag_recv.at[2 * l])
        g_two = Gather(p, xn2.at[l], block, ag_send.at[2 * l + 1], ag_recv.at[2 * l + 1])
        rs = [
            Scatter(
                p, sbuf, rbuf, ysend, yrecv, acc,
                rs_send.at[2 * l + i], rs_recv.at[2 * l + i],
            )
            for i in range(2)
        ]
        save_at = saves(l)
        save_at[7].start()
        norm_into(l, hid, xn1, 0)
        g_one.start()

        @pl.when(l == 0)
        def _():
            for u in range(UNITS, unit_count):
                prepare(u)

        @pl.when(l > 0)
        def _():
            own_copy(l).start()

        pumps(l, *PUMPS[0])
        own_copy(l).wait()

        def project(index):
            at = rows_of(index, block)
            qkv[l, at, :] = mm_nn(xn1[l, at, :], w[l, :, cols_qkv]).astype(BF16)

        g_one.wait_chip()
        g_one.forward()
        need(l, 0, 3)
        project(p.seq_at(0, 0))
        project(p.seq_at(0, 1))
        pumps(l, *PUMPS[1])
        g_one.wait_rest()
        save_at[0].start()
        for k in range(1, yn):
            project(p.seq_at(-k, 0))
            project(p.seq_at(-k, 1))
        save_at[2].start()
        attention(l)
        save_at[3].start()
        save_at[4].start()
        pumps(l, *PUMPS[2])
        need(l, 3, 4)
        rs[0].start(lambda b: mm_nt(ctx[l, rows_of(b, block), :], w[l, :, cols_o]))
        pumps(l, *PUMPS[3])
        rs[0].wait()

        def add_middle(at):
            mid[l, at, :] = hid[l, at, :] + rs[0].rows(at)

        row_loop(block, 32, add_middle)
        save_at[8].start()
        norm_into(l, mid, xn2, 2)
        g_two.start()
        pumps(l, *PUMPS[4])
        need(l, 4, 8)

        def expand(index):
            base = pl.multiple_of(index * block, block)
            upper[...] = mm_nn(xn2[l, pl.ds(base, block), :], w[l, :, cols_up])

            def one(i, unused):
                u = upper[rows_of(i, 16), :]
                at = pl.ds(pl.multiple_of(base + i * 16, 16), 16)
                square = u * u
                t = jnp.tanh(GELU_A * u * (1.0 + GELU_B * square))
                half = 0.5 * (1.0 + t)
                act[l, at, :] = (u * half).astype(BF16)
                slope = (0.5 * GELU_A) * u * (1.0 - t * t) * (1.0 + (3.0 * GELU_B) * square)
                dact[l, at, :] = (half + slope).astype(BF16)
                return unused

            lax.fori_loop(0, block // 16, one, 0)

        expand(p.seq_at(0, 0))
        g_two.wait_chip()
        expand(p.seq_at(0, 1))
        pumps(l, *PUMPS[5])
        g_two.forward()
        pumps(l, *PUMPS[6])
        g_two.wait_rest()
        save_at[1].start()
        for k in range(1, yn):
            expand(p.seq_at(-k, 0))
            expand(p.seq_at(-k, 1))
        save_at[5].start()
        save_at[6].start()
        pumps(l, *PUMPS[7])
        need(l, 8, 12)
        save_weight(l).start()
        rs[1].start(lambda b: mm_nt(act[l, rows_of(b, block), :], w[l, :, cols_down]))
        pumps(l, *PUMPS[8])
        rs[1].wait()

        @pl.when(l < last)
        def _():
            def add_next(at):
                hid[l + 1, at, :] = mid[l, at, :] + rs[1].rows(at)

            row_loop(block, 32, add_next)

        @pl.when(l == last)
        def _():
            def add_out(at):
                out[at, :] = mid[l, at, :] + rs[1].rows(at)

            row_loop(block, 32, add_out)

        return unused

    lax.fori_loop(0, layers, layer, 0)

    def finish(l, unused):
        finish_weight(l)
        for item in saves(l):
            item.wait()
        return unused

    lax.fori_loop(0, layers, finish, 0)


def run_forward(dims, lengths, x_in, norm_in, masters):
    (layers, slots, width, block, local_width, local_ff, groups, zn, xn, yn) = dims
    shard = width // groups
    slot_count, sem_count = sum_slots(zn, xn, yn)

    def saved(*shape, dtype=BF16):
        return jax.ShapeDtypeStruct((layers,) + shape, dtype)

    vmem = pl.BlockSpec(memory_space=pltpu.VMEM)
    smem = pl.BlockSpec(memory_space=pltpu.SMEM)
    hbm = pl.BlockSpec(memory_space=pl.ANY)
    kept = [
        saved(width, UNITS * local_width),
        saved(slots, width),
        saved(slots, width),
        saved(slots, 3 * local_width),
        saved(slots, local_width),
        saved(slots, 128, dtype=F32),
        saved(slots, local_ff),
        saved(slots, local_ff),
        saved(block, width, dtype=F32),
        saved(block, width, dtype=F32),
    ]
    dma = pltpu.SemaphoreType.DMA
    return pl.pallas_call(
        functools.partial(forward_kernel, dims),
        out_shape=[
            jax.ShapeDtypeStruct((block, width), F32),
            jax.ShapeDtypeStruct((4 * layers, width), F32),
        ]
        + kept,
        in_specs=[smem] + [vmem] * 6,
        out_specs=[vmem, vmem] + [hbm] * len(kept),
        scratch_shapes=[pltpu.VMEM(k.shape, k.dtype) for k in kept]
        + [
            pltpu.VMEM((block, local_ff), F32),
            pltpu.VMEM((layers, shard, UNITS * local_width), BF16),
            pltpu.VMEM((4 * layers, width), F32),
            pltpu.VMEM((yn, block, width), BF16),
            pltpu.VMEM((yn, block, width), BF16),
            pltpu.VMEM((yn - 1, block, width), BF16),
            pltpu.VMEM((yn - 1, block, width), BF16),
            pltpu.VMEM((block, width), F32),
            pltpu.VMEM((slot_count, 4 * layers, width), F32),
            dma((UNITS * layers, zn - 1)),
            dma((UNITS * layers, zn - 1)),
            dma((UNITS * layers, xn - 1, zn)),
            dma((UNITS * layers, xn - 1, zn)),
            dma((layers,)),
            dma((layers,)),
            dma((2 * layers, 2 * yn - 1)),
            dma((2 * layers, 2 * yn - 1)),
            dma((2 * layers, 2 * yn - 1)),
            dma((2 * layers, 2 * yn - 1)),
            dma((sem_count,)),
            dma((sem_count,)),
            dma((layers, 9)),
        ],
        compiler_params=pltpu.CompilerParams(
            collective_id=0, has_side_effects=True, vmem_limit_bytes=62 * 2**20
        ),
        name="forward_layers",
    )(lengths, x_in, norm_in, *masters)

def backward_kernel(dims, *refs):
    (layers, slots, width, block, local_width, local_ff, groups, zn, xn, yn) = dims
    heads = local_width // HD
    shard = width // groups
    refs = list(refs)

    def take(count):
        out = refs[:count]
        del refs[:count]
        return out

    lengths, g_in, norms = take(3)
    kept = take(10)
    g_out, norm_grad, total_out = take(3)
    shards = take(1)[0]
    held = take(10)
    w, xn1, xn2, qkv, ctx, lse, act, dact, hid, mid = held
    gfull, gbfull, gctx, dqkv, dk, dv, g, gm, npart = take(9)
    dw, xland, zland = take(3)
    sbuf, rbuf, ysend, yrecv, acc, nslots, tslots = take(7)
    zsend, zrecv, xsend, xrecv = take(4)
    ag_send, ag_recv, rs_send, rs_recv, ns_send, ns_recv, ts_send, ts_recv, load_sem = take(9)

    p = Place(zn, xn, yn)
    length = lengths[0]
    first = p.seq * block
    gu = dact
    w_all = kept[0]

    slopes = [slope_at(p.seq * heads + h) for h in range(heads)]
    weight_at = weight_cols(local_width)
    cols_qkv, cols_o, cols_up, cols_down = weight_at

    def load(l, which):
        if which < 4:
            cols = weight_at[which]
            return pltpu.make_async_copy(w_all.at[l, :, cols], w.at[:, cols], load_sem.at[which])
        return pltpu.make_async_copy(kept[which - 3].at[l], held[which - 3], load_sem.at[which])

    def rows_at(dz, dx):
        return rows_of(p.dp_at(dz, dx), shard)

    def unit_cols(v):
        return pl.ds(v * local_width, local_width)

    def x_copy(l, v, zi, dx):
        cols = unit_cols(v)
        return remote(
            dw.at[rows_at(zi, dx), cols],
            xland.at[l, dx - 1, zi, :, cols],
            xsend.at[l, v, dx - 1, zi],
            xrecv.at[l, v, dx - 1, zi],
            p.dev(dx=dx),
        )

    def z_copy(l, v, zi):
        cols = unit_cols(v)
        return remote(
            dw.at[rows_at(zi, 0), cols],
            zland.at[l, zi - 1, :, cols],
            zsend.at[l, v, zi - 1],
            zrecv.at[l, v, zi - 1],
            p.dev(dz=zi),
        )

    z_order = near_first(zn)
    zi_order = z_order[::-1] + [0]

    def weight_grad(left, right, low, count):
        def one(i, unused):
            at = rows_of(i, 256)
            dw[at, pl.ds(low * local_width, count * local_width)] = mm_tn(
                left[:, at], right[...]
            ).astype(BF16)
            return unused

        lax.fori_loop(0, width // 256, one, 0)

    def send_x(l, *units):
        for v in units:
            for zi in zi_order:
                for dx in range(1, xn):
                    x_copy(l, v, zi, dx).start()

    def reduce_x(l, *units):
        for v in units:
            cols = unit_cols(v)
            for zi in zi_order:
                for dx in range(1, xn):
                    x_copy(l, v, zi, dx).wait_recv()
                base = pl.multiple_of(p.dp_at(zi, 0) * shard, shard)

                def one(i, unused, zi=zi, cols=cols, base=base):
                    here = rows_of(i, 32)
                    at = pl.ds(pl.multiple_of(base + i * 32, 32), 32)
                    value = dw[at, cols].astype(F32)
                    for dx in range(1, xn):
                        value = value + xland[l, dx - 1, zi, here, cols].astype(F32)
                    if zi:
                        dw[at, cols] = value.astype(BF16)
                    else:
                        shards[l, here, cols] = value
                    return unused

                lax.fori_loop(0, shard // 32, one, 0)
                if zi:
                    z_copy(l, v, zi).start()

    def reduce_z(l, low, high):
        def unit(v, unused):
            cols = pl.ds(pl.multiple_of(v * local_width, local_width), local_width)
            here = dw.at[pl.ds(0, shard), pl.ds(0, local_width)]
            for zi in z_order:
                remote(
                    here, here, zsend.at[l, v, zi - 1], zrecv.at[l, v, zi - 1], p.dev(dz=zi)
                ).wait_recv()

            def one(at):
                value = shards[l, at, cols]
                for zi in range(1, zn):
                    value = value + zland[l, zi - 1, at, cols].astype(F32)
                shards[l, at, cols] = value

            row_loop(shard, 32, one)
            for zi in z_order:
                remote(
                    here, here, zsend.at[l, v, zi - 1], zrecv.at[l, v, zi - 1], p.dev(dz=zi)
                ).wait_send()
            for zi in range(zn):
                for dx in range(1, xn):
                    remote(
                        here,
                        here,
                        xsend.at[l, v, dx - 1, zi],
                        xrecv.at[l, v, dx - 1, zi],
                        p.dev(dx=dx),
                    ).wait_send()
            return unused

        lax.fori_loop(low, high, unit, 0)

    def norm_back(l, source, rs, base, row, target, low):
        gain = norms[pl.ds(4 * l + row, 1), :]
        zero = jnp.zeros((8, width), F32)

        def one(i, carry):
            at = rows_of(i, 32)
            scaled, inverse = normalise(source[at, :])
            e = rs.rows(at)
            eg = e * gain
            part = inverse * (
                eg
                - jnp.mean(eg, axis=-1, keepdims=True)
                - scaled * jnp.mean(eg * scaled, axis=-1, keepdims=True)
            )
            value = base[at, :] + part
            target[at, :] = value
            if low is not None:
                low[pl.ds(pl.multiple_of(first + i * 32, 32), 32), :] = value.astype(BF16)
            es = e * scaled
            gains, biases = carry
            for r in range(4):
                gains = gains + es[r * 8 : r * 8 + 8]
                biases = biases + e[r * 8 : r * 8 + 8]
            return gains, biases

        gains, biases = lax.fori_loop(0, block // 32, one, (zero, zero))
        npart[pl.ds(4 * l + row, 1), :] = jnp.sum(gains, axis=0, keepdims=True)
        npart[pl.ds(4 * l + row + 1, 1), :] = jnp.sum(biases, axis=0, keepdims=True)

    def attention(between):
        key_at = lax.broadcasted_iota(jnp.int32, (1, slots), 1)
        step = 256
        causal = lax.broadcasted_iota(jnp.int32, (step, step), 1) <= lax.broadcasted_iota(
            jnp.int32, (step, step), 0
        )
        for h in range(heads):
            bias = jnp.where(key_at < length, slopes[h] * key_at.astype(F32), -jnp.inf)
            cols = pl.ds(h * HD, HD)
            k_cols = pl.ds(local_width + h * HD, HD)
            v_cols = pl.ds(2 * local_width + h * HD, HD)
            for b in range(slots // step):
                here = pl.ds(b * step, step)
                before = pl.ds(0, b * step)
                q = qkv[here, cols]
                gc = gctx[here, cols]
                shift = lse[here, pl.ds(h, 1)]
                raw = mm_nt(q, qkv[here, k_cols]) * SCORE_SCALE + bias[:, b * step : (b + 1) * step]
                p_here = jnp.exp(jnp.where(causal, raw, -jnp.inf) - shift)
                dp_here = mm_nt(gc, qkv[here, v_cols])
                delta = jnp.sum(p_here * dp_here, axis=1, keepdims=True)
                dv[here, :] = mm_tn(p_here.astype(BF16), gc)
                if b:
                    past = mm_nt(q, qkv[before, k_cols]) * SCORE_SCALE + bias[:, : b * step]
                    p_past = jnp.exp(past - shift)
                    dp_past = mm_nt(gc, qkv[before, v_cols])
                    delta = delta + jnp.sum(p_past * dp_past, axis=1, keepdims=True)
                    dv[before, :] += mm_tn(p_past.astype(BF16), gc)
                ds_here = (p_here * (dp_here - delta)).astype(BF16)
                dq = mm_nn(ds_here, qkv[here, k_cols])
                dk[here, :] = mm_tn(ds_here, q)
                if b:
                    ds_past = (p_past * (dp_past - delta)).astype(BF16)
                    dq = dq + mm_nn(ds_past, qkv[before, k_cols])
                    dk[before, :] += mm_tn(ds_past, q)
                dqkv[here, cols] = (dq * SCORE_SCALE).astype(BF16)
                between(h * (slots // step) + b + 1, heads * (slots // step))

            def store(at):
                dqkv[at, k_cols] = (dk[at, :] * SCORE_SCALE).astype(BF16)
                dqkv[at, v_cols] = dv[at, :].astype(BF16)

            row_loop(slots, 64, store)

    p.barrier()

    def mask_in(i, unused):
        at = rows_of(i, 32)
        slot = first + i * 32 + lax.broadcasted_iota(jnp.int32, (32, 1), 0)
        g[at, :] = jnp.where(slot < length, g_in[at, :].astype(F32), 0.0)
        return unused

    lax.fori_loop(0, block // 32, mask_in, 0)
    load_order = (3, 10, 2, 9, 5, 12, 1, 7, 6, 8, 0, 4, 11)

    def layer(step, unused):
        l = layers - 1 - step
        later = l + 1
        for which in load_order:
            load(l, which).start()
        g_one = Gather(p, gfull, block, ag_send.at[2 * l], ag_recv.at[2 * l])
        g_two = Gather(p, gbfull, block, ag_send.at[2 * l + 1], ag_recv.at[2 * l + 1])
        rs = [
            Scatter(
                p, sbuf, rbuf, ysend, yrecv, acc, rs_send.at[2 * l + i], rs_recv.at[2 * l + i]
            )
            for i in range(2)
        ]

        def low_in(i, unused):
            at = pl.ds(pl.multiple_of(first + i * 32, 32), 32)
            gfull[at, :] = g[rows_of(i, 32), :].astype(BF16)
            return unused

        lax.fori_loop(0, block // 32, low_in, 0)
        g_one.start()

        load(l, 3).wait()
        load(l, 10).wait()

        def upper_grad(index):
            at = rows_of(index, block)
            value = mm_nn(gfull[at, :], w[:, cols_down])
            gu[at, :] = (value * dact[at, :].astype(F32)).astype(BF16)

        upper_grad(p.seq_at(0, 0))
        g_one.wait_chip()
        upper_grad(p.seq_at(0, 1))
        g_one.forward()

        @pl.when(step > 0)
        def _():
            reduce_x(later, 0)

        g_one.wait_rest()
        for k in range(1, yn):
            upper_grad(p.seq_at(-k, 0))
            upper_grad(p.seq_at(-k, 1))
        load(l, 2).wait()
        rs[0].start(lambda b: mm_nt(gu[rows_of(b, block), :], w[:, cols_up]))
        load(l, 9).wait()
        load(l, 5).wait()

        @pl.when(step > 0)
        def _():
            reduce_z(later, 3, 12)

        weight_grad(gfull, act, 8, 4)
        send_x(l, 8, 9, 10)
        weight_grad(xn2, gu, 4, 4)

        @pl.when(step > 0)
        def _():
            reduce_x(later, 1, 2)

        load(l, 12).wait()
        reduce_x(l, 8)
        send_x(l, 11)
        rs[0].wait()
        norm_back(l, mid, rs[0], g, 2, gm, gbfull)
        g_two.start()
        reduce_x(l, 9)
        send_x(l, 4)
        load(l, 1).wait()

        def context_grad(index):
            at = rows_of(index, block)
            gctx[at, :] = mm_nn(gbfull[at, :], w[:, cols_o]).astype(BF16)

        context_grad(p.seq_at(0, 0))
        g_two.wait_chip()
        context_grad(p.seq_at(0, 1))
        reduce_x(l, 10)
        send_x(l, 5)
        g_two.forward()

        @pl.when(step > 0)
        def _():
            reduce_z(later, 0, 3)

        g_two.wait_rest()
        for k in range(1, yn):
            context_grad(p.seq_at(-k, 0))
            context_grad(p.seq_at(-k, 1))
        reduce_x(l, 11)
        send_x(l, 6)
        load(l, 7).wait()
        weight_grad(gbfull, ctx, 3, 1)
        load(l, 6).wait()
        load(l, 8).wait()

        def between(done, count):
            if done == (count * 3) // 8:
                reduce_x(l, 4)
                send_x(l, 7)
            if done == (count * 6) // 8:
                reduce_x(l, 5)
                send_x(l, 3)

        attention(between)
        load(l, 0).wait()
        load(l, 4).wait()

        @pl.when(l == 0)
        def _():
            weight_grad(xn1, dqkv, 0, 3)
            send_x(l, 0)

        reduce_x(l, 6)
        rs[1].start(lambda b: mm_nt(dqkv[rows_of(b, block), :], w[:, cols_qkv]))

        @pl.when(l > 0)
        def _():
            weight_grad(xn1, dqkv, 0, 3)
            send_x(l, 0)

        reduce_x(l, 7)
        send_x(l, 1)
        reduce_x(l, 3)
        send_x(l, 2)
        load(l, 11).wait()
        rs[1].wait()
        norm_back(l, hid, rs[1], gm, 0, g, None)
        return unused

    lax.fori_loop(0, layers, layer, 0)
    reduce_x(0, 0, 1, 2)
    g_out[...] = g[...]
    norm_grad[...] = all_sum(p, npart[...], nslots, ns_send, ns_recv)
    reduce_z(0, 3, 12)
    reduce_z(0, 0, 3)

    def squares(i, total):
        l, at = i // (shard // 8), rows_of(lax.rem(i, shard // 8), 8)
        value = shards[l, at, :]
        value = value * value
        for c in range(UNITS * local_width // 128):
            total = total + value[:, c * 128 : (c + 1) * 128]
        return total

    tile = lax.fori_loop(0, layers * shard // 8, squares, jnp.zeros((8, 128), F32))
    tile = all_sum(p, tile, tslots, ts_send, ts_recv)
    value = norm_grad[...]
    value = value * value
    for c in range(width // 128):
        piece = value[:, c * 128 : (c + 1) * 128]
        for r in range(4 * layers // 8):
            tile = tile + piece[r * 8 : r * 8 + 8]
    total = jnp.sum(jnp.sum(tile, axis=0, keepdims=True), axis=1, keepdims=True)
    total_out[...] = jnp.broadcast_to(jnp.sqrt(total), (8, 128))


def run_backward(dims, lengths, g_in, norms, kept):
    (layers, slots, width, block, local_width, local_ff, groups, zn, xn, yn) = dims
    packed = UNITS * local_width
    shard = width // groups
    slot_count, sem_count = sum_slots(zn, xn, yn)
    vmem = pl.BlockSpec(memory_space=pltpu.VMEM)
    smem = pl.BlockSpec(memory_space=pltpu.SMEM)
    hbm = pl.BlockSpec(memory_space=pl.ANY)
    dma = pltpu.SemaphoreType.DMA
    return pl.pallas_call(
        functools.partial(backward_kernel, dims),
        out_shape=[
            jax.ShapeDtypeStruct((block, width), F32),
            jax.ShapeDtypeStruct((4 * layers, width), F32),
            jax.ShapeDtypeStruct((8, 128), F32),
            jax.ShapeDtypeStruct((layers, shard, packed), F32),
        ],
        in_specs=[smem, vmem, vmem] + [hbm] * len(kept),
        out_specs=[vmem] * 4,
        scratch_shapes=[pltpu.VMEM(k.shape[1:], k.dtype) for k in kept]
        + [
            pltpu.VMEM((slots, width), BF16),
            pltpu.VMEM((slots, width), BF16),
            pltpu.VMEM((slots, local_width), BF16),
            pltpu.VMEM((slots, 3 * local_width), BF16),
            pltpu.VMEM((slots, HD), F32),
            pltpu.VMEM((slots, HD), F32),
            pltpu.VMEM((block, width), F32),
            pltpu.VMEM((block, width), F32),
            pltpu.VMEM((4 * layers, width), F32),
            pltpu.VMEM((width, packed), BF16),
            pltpu.VMEM((layers, xn - 1, zn, shard, packed), BF16),
            pltpu.VMEM((layers, zn - 1, shard, packed), BF16),
            pltpu.VMEM((yn, block, width), BF16),
            pltpu.VMEM((yn, block, width), BF16),
            pltpu.VMEM((yn - 1, block, width), BF16),
            pltpu.VMEM((yn - 1, block, width), BF16),
            pltpu.VMEM((block, width), F32),
            pltpu.VMEM((slot_count, 4 * layers, width), F32),
            pltpu.VMEM((slot_count, 8, 128), F32),
            dma((layers, UNITS, zn - 1)),
            dma((layers, UNITS, zn - 1)),
            dma((layers, UNITS, xn - 1, zn)),
            dma((layers, UNITS, xn - 1, zn)),
            dma((2 * layers, 2 * yn - 1)),
            dma((2 * layers, 2 * yn - 1)),
            dma((2 * layers, 2 * yn - 1)),
            dma((2 * layers, 2 * yn - 1)),
            dma((sem_count,)),
            dma((sem_count,)),
            dma((sem_count,)),
            dma((sem_count,)),
            dma((len(kept) + 3,)),
        ],
        compiler_params=pltpu.CompilerParams(
            collective_id=1, has_side_effects=True, vmem_limit_bytes=62 * 2**20
        ),
        name="backward_layers",
    )(lengths, g_in, norms, *kept)


def adam_kernel(dims, *refs):
    (layers, slots, width, block, local_width, local_ff, groups, zn, xn, yn) = dims
    refs = list(refs)

    def take(count):
        out = refs[:count]
        del refs[:count]
        return out

    total, norm_grad, hidden_in, input_in = take(4)
    grads, masters, firsts, seconds = take(4), take(5), take(5), take(5)
    hidden_out, input_out = take(2)
    grad_out, moment_out, variance_out, new_out, copy_out = (take(5) for unused in range(5))
    factor = CLIP_NORM / jnp.maximum(total[0:1, 0:1], CLIP_NORM)
    fix_one = 1.0 / (1.0 - BETA_ONE**STEP)
    fix_two = 1.0 / (1.0 - BETA_TWO**STEP)

    def update(k, at, grad, decay, rate):
        clipped = grad * factor
        momentum = BETA_ONE * firsts[k][at] + (1.0 - BETA_ONE) * clipped
        variance = BETA_TWO * seconds[k][at] + (1.0 - BETA_TWO) * clipped * clipped
        master = masters[k][at]
        size = momentum * fix_one / (jnp.sqrt(variance * fix_two) + ADAM_EPS)
        if decay:
            size = size + decay * master
        fresh = master - rate * size
        grad_out[k][at] = grad
        moment_out[k][at] = momentum
        variance_out[k][at] = variance
        new_out[k][at] = fresh
        copy_out[k][at] = fresh.astype(BF16)

    def matrix(k, at, grad):
        update(k, at, grad, WEIGHT_DECAY, LEARN_RATE)

    hidden_out[...] = hidden_in[...]
    input_out[...] = input_in[...]
    every = slice(None)
    for part in range(3):
        grad = grads[0][0, :, part * local_width : (part + 1) * local_width]
        matrix(0, (0, part, every, every), grad)
    matrix(1, (0, every, every), grads[1][0].T)

    def up_rows(i, unused):
        at = rows_of(i, 16)
        matrix(2, (0, at, every), grads[2][0, at, :])
        return unused

    lax.fori_loop(0, grads[2].shape[1] // 16, up_rows, 0)
    for c in range(grads[3].shape[2] // 128):
        at = pl.ds(c * 128, 128)
        matrix(3, (0, at, every), grads[3][0, :, at].T)

    @pl.when((pl.program_id(0) == 0) & (pl.program_id(1) == 0))
    def _():
        seq_count = CORES * yn
        piece = width // (groups * seq_count)
        at = (lax.axis_index("dp") * seq_count + lax.axis_index("seq")) * piece
        tile = norm_grad[:, rows_of(at // 128, 128)]
        tile = pltpu.roll(tile, lax.rem(128 - lax.rem(at, 128), 128), 1)[:, :piece]
        for l in range(layers):
            update(4, (l,), tile[4 * l : 4 * l + 4], 0.0, NORM_RATE)


def run_adam(dims, total, norm_grad, hidden, input_grad, grad, masters, firsts, seconds):
    (layers, slots, width, block, local_width, local_ff, groups, zn, xn, yn) = dims
    parts = local_width // 128
    shard = width // groups
    piece = width // (groups * CORES * yn)
    rows = block // (layers * parts)

    def same(shape):
        return pl.BlockSpec(shape, lambda l, b: (0,) * len(shape))

    flat = pl.BlockSpec((rows, width), lambda l, b: (l * parts + b, 0))
    grad_specs = [
        pl.BlockSpec((1, shard // parts, 3 * local_width), lambda l, b: (l, b, 0)),
        pl.BlockSpec((1, shard, 128), lambda l, b: (l, 0, 3 * parts + b)),
        pl.BlockSpec((1, shard // parts, local_ff), lambda l, b: (l, b, 1)),
        pl.BlockSpec((1, shard, local_ff // parts), lambda l, b: (l, 0, 2 * parts + b)),
    ]
    own_specs = [
        pl.BlockSpec((1, 3, shard // parts, local_width), lambda l, b: (l, 0, b, 0)),
        pl.BlockSpec((1, 128, shard), lambda l, b: (l, b, 0)),
        pl.BlockSpec((1, shard // parts, local_ff), lambda l, b: (l, b, 0)),
        pl.BlockSpec((1, local_ff // parts, shard), lambda l, b: (l, b, 0)),
        same((layers, 4, piece)),
    ]

    def shapes(dtype):
        return [jax.ShapeDtypeStruct(m.shape, dtype) for m in masters]

    flat_shape = jax.ShapeDtypeStruct((block, width), F32)
    return pl.pallas_call(
        functools.partial(adam_kernel, dims),
        grid=(layers, parts),
        out_shape=[flat_shape, flat_shape] + shapes(F32) * 4 + shapes(BF16),
        in_specs=[same((8, 128)), same((4 * layers, width)), flat, flat]
        + grad_specs
        + own_specs * 3,
        out_specs=[flat, flat] + own_specs * 5,
        compiler_params=pltpu.CompilerParams(vmem_limit_bytes=60 * 2**20),
        name="adam_update",
    )(total, norm_grad, hidden, input_grad, *([grad] * 4), *masters, *firsts, *seconds)


def body(
    block_input,
    output_grad,
    row_lengths,
    qkv_weight,
    proj_weight,
    up_weight,
    down_weight,
    norm_params,
    qkv_first,
    proj_first,
    up_first,
    down_first,
    norm_first,
    qkv_second,
    proj_second,
    up_second,
    down_second,
    norm_second,
):
    row_count, local_slots, width = block_input.shape
    seq_count = lax.axis_size("seq")
    groups = lax.axis_size("dp")
    layer_count = qkv_weight.shape[0]
    local_width = qkv_weight.shape[3]
    dims = (
        layer_count, local_slots * seq_count, width, local_slots, local_width,
        up_weight.shape[2], groups, ZSIZE, groups // ZSIZE, seq_count // CORES,
    )

    def turned(qkv):
        return jnp.transpose(qkv, (0, 2, 1, 3))

    masters = (turned(qkv_weight), proj_weight, up_weight, down_weight, norm_params)
    firsts = (turned(qkv_first), proj_first, up_first, down_first, norm_first)
    seconds = (turned(qkv_second), proj_second, up_second, down_second, norm_second)
    piece = norm_params.shape[2]
    norm_in = norm_params.astype(BF16).astype(F32).reshape(4 * layer_count, piece)
    norm_in = jnp.pad(norm_in, ((0, 0), (0, 128 - piece)))
    flat = (local_slots, width)
    kept = run_forward(dims, row_lengths, block_input.reshape(flat), norm_in, masters[:4])
    back = run_backward(dims, row_lengths, output_grad.reshape(flat), kept[1], kept[2:])
    outs = run_adam(dims, back[2], back[1], kept[0], back[0], back[3], masters, firsts, seconds)
    whole = (row_count,) + flat
    final = [outs[0].reshape(whole), outs[1].reshape(whole), back[2][0, 0]]
    for group in range(5):
        mine = outs[2 + 5 * group : 7 + 5 * group]
        final += [turned(mine[0])] + list(mine[1:])
    return tuple(final)


def solution(mesh):
    return jax.shard_map(
        body,
        mesh=mesh,
        in_specs=(
            P("dp", "seq", None),
            P("dp", "seq", None),
            P("dp"),
            P(None, "dp", None, "seq"),
            P(None, "seq", "dp"),
            P(None, "dp", "seq"),
            P(None, "seq", "dp"),
            P(None, None, ("dp", "seq")),
            P(None, "dp", None, "seq"),
            P(None, "seq", "dp"),
            P(None, "dp", "seq"),
            P(None, "seq", "dp"),
            P(None, None, ("dp", "seq")),
            P(None, "dp", None, "seq"),
            P(None, "seq", "dp"),
            P(None, "dp", "seq"),
            P(None, "seq", "dp"),
            P(None, None, ("dp", "seq")),
        ),
        out_specs=(
            P("dp", "seq", None),
            P("dp", "seq", None),
            P(),
            P(None, "dp", None, "seq"),
            P(None, "seq", "dp"),
            P(None, "dp", "seq"),
            P(None, "seq", "dp"),
            P(None, None, ("dp", "seq")),
            P(None, "dp", None, "seq"),
            P(None, "seq", "dp"),
            P(None, "dp", "seq"),
            P(None, "seq", "dp"),
            P(None, None, ("dp", "seq")),
            P(None, "dp", None, "seq"),
            P(None, "seq", "dp"),
            P(None, "dp", "seq"),
            P(None, "seq", "dp"),
            P(None, None, ("dp", "seq")),
            P(None, "dp", None, "seq"),
            P(None, "seq", "dp"),
            P(None, "dp", "seq"),
            P(None, "seq", "dp"),
            P(None, None, ("dp", "seq")),
            P(None, "dp", None, "seq"),
            P(None, "seq", "dp"),
            P(None, "dp", "seq"),
            P(None, "seq", "dp"),
            P(None, None, ("dp", "seq")),
        ),
        check_vma=False,
    )
```

profile of v0, /device:TPU:0, one launch (start us, length us, event | category | flops | bytes accessed | tf_op | source)
XLA Modules:
  0.0 434.5 jit_solution(13619506905114464289)
XLA Ops:
  1.3 0.7 convert_element_type.6
  2.0 0.6 pad_convert_fusion.refs_2_
  2.6 200.0 %forward_layers.1 = (f32[256,1024]{1,0:T(8,128)}, f32[8,1024]{1,0:T(8,128)}, bf16[2,1024,3072]{2,1,0:T(8,128)(2,1)}, bf16[2,1024,1024]{2,1,0:T(8,128)(2,1)}, bf1...) custom-call(s32[1]{0:T(128)S(6)} %copy.46.refs_0_, ...), custom_call_target="tpu_custom_call" | custom-call | tf_op jit(solution)/shard_map/forward_layers/pallas_call | solution.py:632
  202.6 218.5 %backward_layers.1 = (f32[256,1024]{1,0:T(8,128)}, f32[8,1024]{1,0:T(8,128)}, f32[8,128]{1,0:T(8,128)}, f32[2,128,3072]{2,1,0:T(8,128)}) custom-call(s32[1]{0:T(128)S(6)} %copy.46.refs_0_, bf16[256,1024]{1,0:T(8,128)(2,1)} %bitcast.18, f32[8,1024]{1,0:T(8,128)} %get-tuple-element.71.refs_2_, bf16[2,1024,3072]{2,1,0:T(8,128)(2,1)} %get-tuple-element.72.refs_3_, ...), custom_call_target="tpu_custom_call" | custom-call | tf_op jit(solution)/shard_map/backward_layers/pallas_call | solution.py:1063
  421.0 1.2 slice.3
  422.2 12.1 %adam_update.1 = (f32[256,1024]{1,0:T(8,128)}, f32[256,1024]{1,0:T(8,128)}, f32[2,3,128,256]{3,2,1,0:T(8,128)}, f32[2,256,128]{2,1,0:T(8,128)}, f32[2,128,1024]{...) custom-call(f32[8,128]{1,0:T(8,128)} %get-tuple-element.82.refs_0_, ...), custom_call_target="tpu_custom_call" | custom-call | tf_op jit(solution)/shard_map/adam_update/pallas_call | solution.py:1208
where the time goes:
time: 435 us; the launch traced here: 434 us
  Pallas kernels  430 us (99%)
    pallas_call x1, Pallas kernels, run_backward(): pl.pallas_call(functools.partial(backward_kernel, dims), out_shape=[jax.S...  218 us
    pallas_call x1, Pallas kernels, run_forward(): pl.pallas_call(functools.partial(forward_kernel, dims), out_shape=[jax.Sh...  200 us
    pallas_call x1, Pallas kernels, run_adam(): pl.pallas_call(functools.partial(adam_kernel, dims), grid=(layers, parts)...  12.1 us

commit v1 on v0

--- a/solution.py
+++ b/solution.py
@@ -25,16 +25,17 @@
 
 UNITS = 12
 DEPTH = 2
+DEEPER = (4, 6)
 PUMPS = (
-    ((0, 1, 2), (15, 16)),
-    ((3,), (17,)),
-    ((4,), ()),
-    ((5, 6), (18, 19)),
-    ((7,), (20, 21)),
-    ((8,), ()),
-    ((9,), (22,)),
-    ((10, 11), (23,)),
-    ((12, 13, 14), ()),
+    ((0, 1, 2), (16, 17)),
+    ((3,), (18,)),
+    ((4,), (19,)),
+    ((5, 6), (20, 21)),
+    ((7,), (22,)),
+    ((8,), (23,)),
+    ((9,), ()),
+    ((10, 11), ()),
+    ((12, 13, 14, 15), ()),
 )
 
 F32 = jnp.float32
@@ -47,6 +48,10 @@
 
 def slope_table(head_count):
     return np.power(2.0, -8.0 * (np.arange(head_count) + 1.0) / head_count)
+
+
+def ahead(u):
+    return u + 1 + DEPTH + sum(u >= step for step in DEEPER)
 
 
 def slope_at(head):
@@ -110,16 +115,25 @@
         core = (1 - self.c) if dc else self.c
         return self.yo(dy) * CORES + core
 
-    def peers(self):
+    def seq_others(self):
+        return [(y, c) for c in range(CORES) for y in range(self.yn) if y or c]
+
+    def dp_others(self):
+        return [(z, x) for x in range(self.xn) for z in range(self.zn) if z or x]
+
+    def peers(self, wide=False):
+        if wide:
+            out = [self.dev(dy=y, dc=c) for y, c in self.seq_others()]
+            return out + [self.dev(dz=z, dx=x) for z, x in self.dp_others()]
         out = [self.dev(dc=1)]
         out += [self.dev(dy=k) for k in range(1, self.yn)]
         out += [self.dev(dx=k) for k in range(1, self.xn)]
         out += [self.dev(dz=k) for k in range(1, self.zn)]
         return out
 
-    def barrier(self):
+    def barrier(self, wide=False):
         sem = pltpu.get_barrier_semaphore()
-        peers = self.peers()
+        peers = self.peers(wide)
         for peer in peers:
             pl.semaphore_signal(sem, inc=1, device_id=peer, device_id_type=MESH)
         pl.semaphore_wait(sem, len(peers))
@@ -169,6 +183,32 @@
     return CORES + yn + xn + zn, 1 + (yn - 1) + (xn - 1) + (zn - 1)
 
 
+def all_sum_wide(place, value, slots, send, recv):
+    p = place
+    stages = (
+        (p.seq, [(p.dev(dy=y, dc=c), p.seq_at(-y, c)) for y, c in p.seq_others()]),
+        (p.dp, [(p.dev(dz=z, dx=x), p.dp_at(-z, -x)) for z, x in p.dp_others()]),
+    )
+    base = 0
+    at = 0
+    for mine, others in stages:
+        slots[base + mine] = value
+        own = slots.at[base + mine]
+        for k, (target, origin) in enumerate(others):
+            remote(own, own, send.at[at + k], recv.at[at + k], target).start()
+        for k, (target, origin) in enumerate(others):
+            came = slots.at[base + origin]
+            remote(came, came, send.at[at + k], recv.at[at + k], target).wait_recv()
+        for k, (target, origin) in enumerate(others):
+            remote(own, own, send.at[at + k], recv.at[at + k], target).wait_send()
+        value = slots[base]
+        for k in range(len(others)):
+            value = value + slots[base + k + 1]
+        base += len(others) + 1
+        at += len(others)
+    return value
+
+
 class Gather:
     def __init__(self, place, buf, block, send, recv):
         self.p, self.buf, self.block, self.send, self.recv = place, buf, block, send, recv
@@ -268,10 +308,28 @@
     lax.fori_loop(0, total // step, one, 0)
 
 
+def twice(v):
+    return jnp.concatenate([v, v], axis=1)
+
+
+def key_bias(bias, slots, length, slope):
+    def one(i, unused):
+        key = i * 64 + lax.broadcasted_iota(jnp.int32, (64, 128), 0)
+        bias[rows_of(i, 64), :] = jnp.where(key < length, slope * key.astype(F32), -jnp.inf)
+        return unused
+
+    lax.fori_loop(0, slots // 64, one, 0)
+
+
+def turn_rows(target, rows, slots):
+    for c in range(slots // 256):
+        at = pl.ds(c * 256, 256)
+        target[:, at] = rows(at).astype(F32).T.astype(BF16)
+
+
 def forward_kernel(dims, *refs):
     (layers, slots, width, block, local_width, local_ff, groups, zn, xn, yn) = dims
     heads = local_width // HD
-    shard = width // groups
     refs = list(refs)
 
     def take(count):
@@ -285,9 +343,9 @@
     w_save = take(1)[0]
     xn1_save, xn2_save, qkv_save, ctx_save, lse_save, act_save, dact_save, hid_save, mid_save = take(9)
     w = take(1)[0]
-    xn1, xn2, qkv, ctx, lse, act, dact, hid, mid, upper, ws, norm_place = take(12)
+    xn1, xn2, qkv, ctx, lse, act, dact, hid, mid, upper, norm_place, bias, turned = take(13)
     sbuf, rbuf, ysend, yrecv, acc, nslots = take(6)
-    zsend, zrecv, xsend, xrecv, own_sem, wsave_sem = take(6)
+    zsend, zrecv, xsend, xrecv, wsave_sem = take(5)
     ag_send, ag_recv, rs_send, rs_recv, ns_send, ns_recv, save_sem = take(7)
 
     p = Place(zn, xn, yn)
@@ -298,62 +356,44 @@
     unit_count = UNITS * layers
     slopes = [slope_at(p.seq * heads + h) for h in range(heads)]
 
-    def shard_rows(index):
-        return rows_of(index, shard)
-
     def unit_cols(u):
         return pl.ds((u % UNITS) * local_width, local_width)
 
-    def z_copy(u, dz, origin):
-        l, cols = u // UNITS, unit_cols(u)
-        return remote(
-            ws.at[l, :, cols],
-            w.at[l, shard_rows(origin), cols],
-            zsend.at[u, dz - 1],
-            zrecv.at[u, dz - 1],
-            p.dev(dz=dz),
-        )
-
-    def x_copy(u, dx, dz, origin):
-        l, cols = u // UNITS, unit_cols(u)
-        there = w.at[l, shard_rows(origin), cols]
-        return remote(
-            there if dz else ws.at[l, :, cols],
-            there,
-            xsend.at[u, dx - 1, dz],
-            xrecv.at[u, dx - 1, dz],
-            p.dev(dx=dx),
-        )
-
-    def own_copy(l):
-        return pltpu.make_async_copy(ws.at[l], w.at[l, shard_rows(p.dp)], own_sem.at[l])
+    def z_copy(u, dz, zi):
+        here = w.at[u // UNITS, zi, p.x, :, unit_cols(u)]
+        return remote(here, here, zsend.at[u, dz - 1], zrecv.at[u, dz - 1], p.dev(dz=dz))
+
+    def x_copy(u, dx, dz):
+        here = w.at[u // UNITS, p.zo(-dz), p.x, :, unit_cols(u)]
+        return remote(here, here, xsend.at[u, dx - 1, dz], xrecv.at[u, dx - 1, dz], p.dev(dx=dx))
 
     def prepare(u):
         l, v = divmod(u, UNITS)
         cols = unit_cols(u)
         if v < 3:
-            ws[l, :, cols] = masters[0][l, v].astype(BF16)
+            w[l, p.z, p.x, :, cols] = masters[0][l, v].astype(BF16)
         elif 4 <= v < 8:
-            ws[l, :, cols] = masters[2][l, :, pl.ds((v - 4) * local_width, local_width)].astype(BF16)
+            source = pl.ds((v - 4) * local_width, local_width)
+            w[l, p.z, p.x, :, cols] = masters[2][l, :, source].astype(BF16)
         else:
             source, base = (masters[1], 0) if v == 3 else (masters[3], (v - 8) * local_width)
             for c in range(local_width // 128):
-                turned = source[l, pl.ds(base + c * 128, 128), :].T
-                ws[l, :, pl.ds((v % UNITS) * local_width + c * 128, 128)] = turned.astype(BF16)
+                block_t = source[l, pl.ds(base + c * 128, 128), :].T
+                w[l, p.z, p.x, :, pl.ds(v * local_width + c * 128, 128)] = block_t.astype(BF16)
 
     def start_unit(u):
         for dz in z_order:
-            z_copy(u, dz, p.dp).start()
+            z_copy(u, dz, p.z).start()
         for dx in range(1, xn):
-            x_copy(u, dx, 0, p.dp).start()
+            x_copy(u, dx, 0).start()
 
     def pump(u):
         for dz in z_order:
-            z_copy(u, dz, p.dp_at(-dz, 0)).wait_recv()
+            z_copy(u, dz, p.zo(-dz)).wait_recv()
             for dx in range(1, xn):
-                x_copy(u, dx, dz, p.dp_at(-dz, 0)).start()
-        if u + DEPTH < unit_count:
-            start_unit(u + DEPTH)
+                x_copy(u, dx, dz).start()
+        for later in range(ahead(u - 1), min(ahead(u), unit_count)):
+            start_unit(later)
 
     def pumps(l, *tables):
         for at, units in enumerate(tables):
@@ -370,9 +410,9 @@
     def need(l, low, high):
         def one(v, unused):
             u = UNITS * l + v
+            at = w.at[0, 0, 0, :, pl.ds(0, local_width)]
             for dz in range(zn):
                 for dx in range(1, xn):
-                    at = w.at[0, shard_rows(p.dp_at(-dz, -dx)), pl.ds(0, local_width)]
                     remote(
                         at, at, xsend.at[u, dx - 1, dz], xrecv.at[u, dx - 1, dz], p.dev(dx=dx)
                     ).wait_recv()
@@ -383,7 +423,7 @@
     def finish_weight(l):
         def one(v, unused):
             u = UNITS * l + v
-            at = ws.at[0, :, pl.ds(0, local_width)]
+            at = w.at[0, 0, 0, :, pl.ds(0, local_width)]
             for dz in z_order:
                 remote(
                     at, at, zsend.at[u, dz - 1], zrecv.at[u, dz - 1], p.dev(dz=dz)
@@ -397,6 +437,9 @@
 
         lax.fori_loop(0, UNITS, one, 0)
         save_weight(l).wait()
+
+    def weight(l, cols):
+        return w[l, :, :, :, cols].reshape(width, cols.size)
 
     def save(l, which, src, dst):
         return pltpu.make_async_copy(src, dst, save_sem.at[l, which])
@@ -415,7 +458,7 @@
         )
 
     p.barrier()
-    for u in range(DEPTH):
+    for u in range(ahead(-1)):
         prepare(u)
         start_unit(u)
     piece = width // (groups * CORES * yn)
@@ -423,9 +466,8 @@
     norm_place[...] = jnp.zeros_like(norm_place)
     norm_place[:, rows_of(at_lane // 128, 128)] = pltpu.roll(norm_in[...], lax.rem(at_lane, 128), 1)
     norm_out[...] = all_sum(p, norm_place[...], nslots, ns_send, ns_recv)
-    for u in range(DEPTH, UNITS):
+    for u in range(ahead(-1), UNITS):
         prepare(u)
-    own_copy(0).start()
 
     def load_in(at):
         hid[0, at, :] = x_in[at, :].astype(F32)
@@ -448,35 +490,35 @@
         lax.fori_loop(0, block // 32, one, 0)
 
     def attention(l):
-        key_at = lax.broadcasted_iota(jnp.int32, (1, slots), 1)
         step = 256
-        causal = lax.broadcasted_iota(jnp.int32, (step, step), 1) <= lax.broadcasted_iota(
-            jnp.int32, (step, step), 0
+        causal = lax.broadcasted_iota(jnp.int32, (step, step), 0) <= lax.broadcasted_iota(
+            jnp.int32, (step, step), 1
         )
         for h in range(heads):
-            bias = jnp.where(key_at < length, slopes[h] * key_at.astype(F32), -jnp.inf)
             cols = pl.ds(h * HD, HD)
+            k_cols = pl.ds(local_width + h * HD, HD)
+            v_cols = pl.ds(2 * local_width + h * HD, HD)
+            key_bias(bias, slots, length, slopes[h])
+            turn_rows(turned, lambda at: qkv[l, at, v_cols], slots)
             for b in range(slots // step):
                 here = pl.ds(b * step, step)
                 before = pl.ds(0, b * step)
-                k_cols = pl.ds(local_width + h * HD, HD)
-                v_cols = pl.ds(2 * local_width + h * HD, HD)
                 q = qkv[l, here, cols]
-                raw = mm_nt(q, qkv[l, here, k_cols]) * SCORE_SCALE + bias[:, b * step : (b + 1) * step]
+                raw = mm_nt(qkv[l, here, k_cols], q) * SCORE_SCALE + twice(bias[here, :])
                 raw = jnp.where(causal, raw, -jnp.inf)
-                top = jnp.max(raw, axis=1, keepdims=True)
+                top = jnp.max(raw, axis=0, keepdims=True)
                 if b:
-                    past = mm_nt(q, qkv[l, before, k_cols]) * SCORE_SCALE + bias[:, : b * step]
-                    top = jnp.maximum(top, jnp.max(past, axis=1, keepdims=True))
+                    past = mm_nt(qkv[l, before, k_cols], q) * SCORE_SCALE + twice(bias[before, :])
+                    top = jnp.maximum(top, jnp.max(past, axis=0, keepdims=True))
                 e_here = jnp.exp(raw - top)
-                total = jnp.sum(e_here, axis=1, keepdims=True)
-                value = mm_nn(e_here.astype(BF16), qkv[l, here, v_cols])
+                total = jnp.sum(e_here, axis=0, keepdims=True)
+                value = mm_nn(turned[:, here], e_here.astype(BF16))
                 if b:
                     e_past = jnp.exp(past - top)
-                    total = total + jnp.sum(e_past, axis=1, keepdims=True)
-                    value = value + mm_nn(e_past.astype(BF16), qkv[l, before, v_cols])
-                ctx[l, here, cols] = (value / total).astype(BF16)
-                lse[l, here, pl.ds(h, 1)] = top + jnp.log(total)
+                    total = total + jnp.sum(e_past, axis=0, keepdims=True)
+                    value = value + mm_nn(turned[:, before], e_past.astype(BF16))
+                ctx[l, here, cols] = (value / total).T.astype(BF16)
+                lse[l, pl.ds(h, 1), here] = top + jnp.log(total)
 
     def layer(l, unused):
         last = layers - 1
@@ -499,16 +541,11 @@
             for u in range(UNITS, unit_count):
                 prepare(u)
 
-        @pl.when(l > 0)
-        def _():
-            own_copy(l).start()
-
         pumps(l, *PUMPS[0])
-        own_copy(l).wait()
 
         def project(index):
             at = rows_of(index, block)
-            qkv[l, at, :] = mm_nn(xn1[l, at, :], w[l, :, cols_qkv]).astype(BF16)
+            qkv[l, at, :] = mm_nn(xn1[l, at, :], weight(l, cols_qkv)).astype(BF16)
 
         g_one.wait_chip()
         g_one.forward()
@@ -527,7 +564,7 @@
         save_at[4].start()
         pumps(l, *PUMPS[2])
         need(l, 3, 4)
-        rs[0].start(lambda b: mm_nt(ctx[l, rows_of(b, block), :], w[l, :, cols_o]))
+        rs[0].start(lambda b: mm_nt(ctx[l, rows_of(b, block), :], weight(l, cols_o)))
         pumps(l, *PUMPS[3])
         rs[0].wait()
 
@@ -543,7 +580,7 @@
 
         def expand(index):
             base = pl.multiple_of(index * block, block)
-            upper[...] = mm_nn(xn2[l, pl.ds(base, block), :], w[l, :, cols_up])
+            upper[...] = mm_nn(xn2[l, pl.ds(base, block), :], weight(l, cols_up))
 
             def one(i, unused):
                 u = upper[rows_of(i, 16), :]
@@ -574,7 +611,7 @@
         pumps(l, *PUMPS[7])
         need(l, 8, 12)
         save_weight(l).start()
-        rs[1].start(lambda b: mm_nt(act[l, rows_of(b, block), :], w[l, :, cols_down]))
+        rs[1].start(lambda b: mm_nt(act[l, rows_of(b, block), :], weight(l, cols_down)))
         pumps(l, *PUMPS[8])
         rs[1].wait()
 
@@ -617,12 +654,12 @@
     smem = pl.BlockSpec(memory_space=pltpu.SMEM)
     hbm = pl.BlockSpec(memory_space=pl.ANY)
     kept = [
-        saved(width, UNITS * local_width),
+        saved(zn, xn, shard, UNITS * local_width),
         saved(slots, width),
         saved(slots, width),
         saved(slots, 3 * local_width),
         saved(slots, local_width),
-        saved(slots, 128, dtype=F32),
+        saved(8, slots, dtype=F32),
         saved(slots, local_ff),
         saved(slots, local_ff),
         saved(block, width, dtype=F32),
@@ -641,8 +678,9 @@
         scratch_shapes=[pltpu.VMEM(k.shape, k.dtype) for k in kept]
         + [
             pltpu.VMEM((block, local_ff), F32),
-            pltpu.VMEM((layers, shard, UNITS * local_width), BF16),
             pltpu.VMEM((4 * layers, width), F32),
+            pltpu.VMEM((slots, 128), F32),
+            pltpu.VMEM((HD, slots), BF16),
             pltpu.VMEM((yn, block, width), BF16),
             pltpu.VMEM((yn, block, width), BF16),
             pltpu.VMEM((yn - 1, block, width), BF16),
@@ -653,7 +691,6 @@
             dma((UNITS * layers, zn - 1)),
             dma((UNITS * layers, xn - 1, zn)),
             dma((UNITS * layers, xn - 1, zn)),
-            dma((layers,)),
             dma((layers,)),
             dma((2 * layers, 2 * yn - 1)),
             dma((2 * layers, 2 * yn - 1)),
@@ -673,6 +710,7 @@
     (layers, slots, width, block, local_width, local_ff, groups, zn, xn, yn) = dims
     heads = local_width // HD
     shard = width // groups
+    slab = shard * xn
     refs = list(refs)
 
     def take(count):
@@ -686,7 +724,7 @@
     shards = take(1)[0]
     held = take(10)
     w, xn1, xn2, qkv, ctx, lse, act, dact, hid, mid = held
-    gfull, gbfull, gctx, dqkv, dk, dv, g, gm, npart = take(9)
+    gfull, gbfull, gctx, dqkv, dk, dv, bias, turned, g, gm, npart = take(11)
     dw, xland, zland = take(3)
     sbuf, rbuf, ysend, yrecv, acc, nslots, tslots = take(7)
     zsend, zrecv, xsend, xrecv = take(4)
@@ -705,29 +743,29 @@
     def load(l, which):
         if which < 4:
             cols = weight_at[which]
-            return pltpu.make_async_copy(w_all.at[l, :, cols], w.at[:, cols], load_sem.at[which])
+            return pltpu.make_async_copy(w_all.at[l, :, :, :, cols], w.at[:, :, :, cols], load_sem.at[which])
         return pltpu.make_async_copy(kept[which - 3].at[l], held[which - 3], load_sem.at[which])
 
-    def rows_at(dz, dx):
-        return rows_of(p.dp_at(dz, dx), shard)
+    def weight(cols):
+        return w[:, :, :, cols].reshape(width, cols.size)
 
     def unit_cols(v):
         return pl.ds(v * local_width, local_width)
 
-    def x_copy(l, v, zi, dx):
+    def x_copy(l, v, dx):
         cols = unit_cols(v)
         return remote(
-            dw.at[rows_at(zi, dx), cols],
-            xland.at[l, dx - 1, zi, :, cols],
-            xsend.at[l, v, dx - 1, zi],
-            xrecv.at[l, v, dx - 1, zi],
+            dw.at[:, p.xo(dx), :, cols],
+            xland.at[l, dx - 1, :, :, cols],
+            xsend.at[l, v, dx - 1],
+            xrecv.at[l, v, dx - 1],
             p.dev(dx=dx),
         )
 
     def z_copy(l, v, zi):
         cols = unit_cols(v)
         return remote(
-            dw.at[rows_at(zi, 0), cols],
+            dw.at[p.zo(zi), p.x, :, cols],
             zland.at[l, zi - 1, :, cols],
             zsend.at[l, v, zi - 1],
             zrecv.at[l, v, zi - 1],
@@ -739,36 +777,34 @@
 
     def weight_grad(left, right, low, count):
         def one(i, unused):
-            at = rows_of(i, 256)
-            dw[at, pl.ds(low * local_width, count * local_width)] = mm_tn(
-                left[:, at], right[...]
-            ).astype(BF16)
+            part = mm_tn(left[:, rows_of(i, slab)], right[...]).astype(BF16)
+            dw[i, :, :, pl.ds(low * local_width, count * local_width)] = part.reshape(
+                xn, shard, count * local_width
+            )
             return unused
 
-        lax.fori_loop(0, width // 256, one, 0)
+        lax.fori_loop(0, zn, one, 0)
 
     def send_x(l, *units):
         for v in units:
-            for zi in zi_order:
-                for dx in range(1, xn):
-                    x_copy(l, v, zi, dx).start()
+            for dx in range(1, xn):
+                x_copy(l, v, dx).start()
 
     def reduce_x(l, *units):
         for v in units:
             cols = unit_cols(v)
+            for dx in range(1, xn):
+                x_copy(l, v, dx).wait_recv()
             for zi in zi_order:
-                for dx in range(1, xn):
-                    x_copy(l, v, zi, dx).wait_recv()
-                base = pl.multiple_of(p.dp_at(zi, 0) * shard, shard)
-
-                def one(i, unused, zi=zi, cols=cols, base=base):
+                zz = p.zo(zi)
+
+                def one(i, unused, zi=zi, cols=cols, zz=zz):
                     here = rows_of(i, 32)
-                    at = pl.ds(pl.multiple_of(base + i * 32, 32), 32)
-                    value = dw[at, cols].astype(F32)
+                    value = dw[zz, p.x, here, cols].astype(F32)
                     for dx in range(1, xn):
-                        value = value + xland[l, dx - 1, zi, here, cols].astype(F32)
+                        value = value + xland[l, dx - 1, zz, here, cols].astype(F32)
                     if zi:
-                        dw[at, cols] = value.astype(BF16)
+                        dw[zz, p.x, here, cols] = value.astype(BF16)
                     else:
                         shards[l, here, cols] = value
                     return unused
@@ -780,7 +816,7 @@
     def reduce_z(l, low, high):
         def unit(v, unused):
             cols = pl.ds(pl.multiple_of(v * local_width, local_width), local_width)
-            here = dw.at[pl.ds(0, shard), pl.ds(0, local_width)]
+            here = dw.at[0, 0, :, pl.ds(0, local_width)]
             for zi in z_order:
                 remote(
                     here, here, zsend.at[l, v, zi - 1], zrecv.at[l, v, zi - 1], p.dev(dz=zi)
@@ -797,15 +833,11 @@
                 remote(
                     here, here, zsend.at[l, v, zi - 1], zrecv.at[l, v, zi - 1], p.dev(dz=zi)
                 ).wait_send()
-            for zi in range(zn):
-                for dx in range(1, xn):
-                    remote(
-                        here,
-                        here,
-                        xsend.at[l, v, dx - 1, zi],
-                        xrecv.at[l, v, dx - 1, zi],
-                        p.dev(dx=dx),
-                    ).wait_send()
+            every = dw.at[:, 0, :, pl.ds(0, local_width)]
+            for dx in range(1, xn):
+                remote(
+                    every, every, xsend.at[l, v, dx - 1], xrecv.at[l, v, dx - 1], p.dev(dx=dx)
+                ).wait_send()
             return unused
 
         lax.fori_loop(low, high, unit, 0)
@@ -840,41 +872,41 @@
         npart[pl.ds(4 * l + row + 1, 1), :] = jnp.sum(biases, axis=0, keepdims=True)
 
     def attention(between):
-        key_at = lax.broadcasted_iota(jnp.int32, (1, slots), 1)
         step = 256
-        causal = lax.broadcasted_iota(jnp.int32, (step, step), 1) <= lax.broadcasted_iota(
-            jnp.int32, (step, step), 0
+        causal = lax.broadcasted_iota(jnp.int32, (step, step), 0) <= lax.broadcasted_iota(
+            jnp.int32, (step, step), 1
         )
         for h in range(heads):
-            bias = jnp.where(key_at < length, slopes[h] * key_at.astype(F32), -jnp.inf)
             cols = pl.ds(h * HD, HD)
             k_cols = pl.ds(local_width + h * HD, HD)
             v_cols = pl.ds(2 * local_width + h * HD, HD)
+            key_bias(bias, slots, length, slopes[h])
+            turn_rows(turned, lambda at: qkv[at, k_cols], slots)
             for b in range(slots // step):
                 here = pl.ds(b * step, step)
                 before = pl.ds(0, b * step)
                 q = qkv[here, cols]
                 gc = gctx[here, cols]
-                shift = lse[here, pl.ds(h, 1)]
-                raw = mm_nt(q, qkv[here, k_cols]) * SCORE_SCALE + bias[:, b * step : (b + 1) * step]
+                shift = lse[pl.ds(h, 1), here]
+                raw = mm_nt(qkv[here, k_cols], q) * SCORE_SCALE + twice(bias[here, :])
                 p_here = jnp.exp(jnp.where(causal, raw, -jnp.inf) - shift)
-                dp_here = mm_nt(gc, qkv[here, v_cols])
-                delta = jnp.sum(p_here * dp_here, axis=1, keepdims=True)
-                dv[here, :] = mm_tn(p_here.astype(BF16), gc)
+                dp_here = mm_nt(qkv[here, v_cols], gc)
+                delta = jnp.sum(p_here * dp_here, axis=0, keepdims=True)
+                dv[here, :] = mm_nn(p_here.astype(BF16), gc)
                 if b:
-                    past = mm_nt(q, qkv[before, k_cols]) * SCORE_SCALE + bias[:, : b * step]
+                    past = mm_nt(qkv[before, k_cols], q) * SCORE_SCALE + twice(bias[before, :])
                     p_past = jnp.exp(past - shift)
-                    dp_past = mm_nt(gc, qkv[before, v_cols])
-                    delta = delta + jnp.sum(p_past * dp_past, axis=1, keepdims=True)
-                    dv[before, :] += mm_tn(p_past.astype(BF16), gc)
+                    dp_past = mm_nt(qkv[before, v_cols], gc)
+                    delta = delta + jnp.sum(p_past * dp_past, axis=0, keepdims=True)
+                    dv[before, :] += mm_nn(p_past.astype(BF16), gc)
                 ds_here = (p_here * (dp_here - delta)).astype(BF16)
-                dq = mm_nn(ds_here, qkv[here, k_cols])
-                dk[here, :] = mm_tn(ds_here, q)
+                dq = mm_nn(turned[:, here], ds_here)
+                dk[here, :] = mm_nn(ds_here, q)
                 if b:
                     ds_past = (p_past * (dp_past - delta)).astype(BF16)
-                    dq = dq + mm_nn(ds_past, qkv[before, k_cols])
-                    dk[before, :] += mm_tn(ds_past, q)
-                dqkv[here, cols] = (dq * SCORE_SCALE).astype(BF16)
+                    dq = dq + mm_nn(turned[:, before], ds_past)
+                    dk[before, :] += mm_nn(ds_past, q)
+                dqkv[here, cols] = (dq * SCORE_SCALE).T.astype(BF16)
                 between(h * (slots // step) + b + 1, heads * (slots // step))
 
             def store(at):
@@ -883,7 +915,7 @@
 
             row_loop(slots, 64, store)
 
-    p.barrier()
+    p.barrier(wide=True)
 
     def mask_in(i, unused):
         at = rows_of(i, 32)
@@ -921,7 +953,7 @@
 
         def upper_grad(index):
             at = rows_of(index, block)
-            value = mm_nn(gfull[at, :], w[:, cols_down])
+            value = mm_nn(gfull[at, :], weight(cols_down))
             gu[at, :] = (value * dact[at, :].astype(F32)).astype(BF16)
 
         upper_grad(p.seq_at(0, 0))
@@ -932,13 +964,14 @@
         @pl.when(step > 0)
         def _():
             reduce_x(later, 0)
+            send_x(later, 2)
 
         g_one.wait_rest()
         for k in range(1, yn):
             upper_grad(p.seq_at(-k, 0))
             upper_grad(p.seq_at(-k, 1))
         load(l, 2).wait()
-        rs[0].start(lambda b: mm_nt(gu[rows_of(b, block), :], w[:, cols_up]))
+        rs[0].start(lambda b: mm_nt(gu[rows_of(b, block), :], weight(cols_up)))
         load(l, 9).wait()
         load(l, 5).wait()
 
@@ -947,8 +980,9 @@
             reduce_z(later, 3, 12)
 
         weight_grad(gfull, act, 8, 4)
-        send_x(l, 8, 9, 10)
+        send_x(l, 8)
         weight_grad(xn2, gu, 4, 4)
+        send_x(l, 9)
 
         @pl.when(step > 0)
         def _():
@@ -956,23 +990,23 @@
 
         load(l, 12).wait()
         reduce_x(l, 8)
-        send_x(l, 11)
+        send_x(l, 10)
         rs[0].wait()
         norm_back(l, mid, rs[0], g, 2, gm, gbfull)
         g_two.start()
         reduce_x(l, 9)
-        send_x(l, 4)
+        send_x(l, 11)
         load(l, 1).wait()
 
         def context_grad(index):
             at = rows_of(index, block)
-            gctx[at, :] = mm_nn(gbfull[at, :], w[:, cols_o]).astype(BF16)
+            gctx[at, :] = mm_nn(gbfull[at, :], weight(cols_o)).astype(BF16)
 
         context_grad(p.seq_at(0, 0))
         g_two.wait_chip()
         context_grad(p.seq_at(0, 1))
         reduce_x(l, 10)
-        send_x(l, 5)
+        send_x(l, 4)
         g_two.forward()
 
         @pl.when(step > 0)
@@ -983,20 +1017,20 @@
         for k in range(1, yn):
             context_grad(p.seq_at(-k, 0))
             context_grad(p.seq_at(-k, 1))
-        reduce_x(l, 11)
-        send_x(l, 6)
         load(l, 7).wait()
         weight_grad(gbfull, ctx, 3, 1)
+        reduce_x(l, 11)
+        send_x(l, 5)
         load(l, 6).wait()
         load(l, 8).wait()
 
         def between(done, count):
             if done == (count * 3) // 8:
                 reduce_x(l, 4)
-                send_x(l, 7)
+                send_x(l, 6)
             if done == (count * 6) // 8:
                 reduce_x(l, 5)
-                send_x(l, 3)
+                send_x(l, 7)
 
         attention(between)
         load(l, 0).wait()
@@ -1005,27 +1039,28 @@
         @pl.when(l == 0)
         def _():
             weight_grad(xn1, dqkv, 0, 3)
-            send_x(l, 0)
 
         reduce_x(l, 6)
-        rs[1].start(lambda b: mm_nt(dqkv[rows_of(b, block), :], w[:, cols_qkv]))
+        send_x(l, 3)
+        rs[1].start(lambda b: mm_nt(dqkv[rows_of(b, block), :], weight(cols_qkv)))
 
         @pl.when(l > 0)
         def _():
             weight_grad(xn1, dqkv, 0, 3)
-            send_x(l, 0)
 
         reduce_x(l, 7)
+        send_x(l, 0)
+        reduce_x(l, 3)
         send_x(l, 1)
-        reduce_x(l, 3)
-        send_x(l, 2)
         load(l, 11).wait()
         rs[1].wait()
         norm_back(l, hid, rs[1], gm, 0, g, None)
         return unused
 
     lax.fori_loop(0, layers, layer, 0)
-    reduce_x(0, 0, 1, 2)
+    reduce_x(0, 0)
+    send_x(0, 2)
+    reduce_x(0, 1, 2)
     g_out[...] = g[...]
     norm_grad[...] = all_sum(p, npart[...], nslots, ns_send, ns_recv)
     reduce_z(0, 3, 12)
@@ -1040,7 +1075,7 @@
         return total
 
     tile = lax.fori_loop(0, layers * shard // 8, squares, jnp.zeros((8, 128), F32))
-    tile = all_sum(p, tile, tslots, ts_send, ts_recv)
+    tile = all_sum_wide(p, tile, tslots, ts_send, ts_recv)
     value = norm_grad[...]
     value = value * value
     for c in range(width // 128):
@@ -1078,10 +1113,12 @@
             pltpu.VMEM((slots, 3 * local_width), BF16),
             pltpu.VMEM((slots, HD), F32),
             pltpu.VMEM((slots, HD), F32),
+            pltpu.VMEM((slots, 128), F32),
+            pltpu.VMEM((HD, slots), BF16),
             pltpu.VMEM((block, width), F32),
             pltpu.VMEM((block, width), F32),
             pltpu.VMEM((4 * layers, width), F32),
-            pltpu.VMEM((width, packed), BF16),
+            pltpu.VMEM((zn, xn, shard, packed), BF16),
             pltpu.VMEM((layers, xn - 1, zn, shard, packed), BF16),
             pltpu.VMEM((layers, zn - 1, shard, packed), BF16),
             pltpu.VMEM((yn, block, width), BF16),
@@ -1090,19 +1127,19 @@
             pltpu.VMEM((yn - 1, block, width), BF16),
             pltpu.VMEM((block, width), F32),
             pltpu.VMEM((slot_count, 4 * layers, width), F32),
-            pltpu.VMEM((slot_count, 8, 128), F32),
+            pltpu.VMEM((CORES * yn + groups, 8, 128), F32),
             dma((layers, UNITS, zn - 1)),
             dma((layers, UNITS, zn - 1)),
-            dma((layers, UNITS, xn - 1, zn)),
-            dma((layers, UNITS, xn - 1, zn)),
+            dma((layers, UNITS, xn - 1)),
+            dma((layers, UNITS, xn - 1)),
             dma((2 * layers, 2 * yn - 1)),
             dma((2 * layers, 2 * yn - 1)),
             dma((2 * layers, 2 * yn - 1)),
             dma((2 * layers, 2 * yn - 1)),
             dma((sem_count,)),
             dma((sem_count,)),
-            dma((sem_count,)),
-            dma((sem_count,)),
+            dma((CORES * yn + groups - 2,)),
+            dma((CORES * yn + groups - 2,)),
             dma((len(kept) + 3,)),
         ],
         compiler_params=pltpu.CompilerParams(

time: 435 us -> 424 us (0.975)
  Pallas kernels: 430 us -> 420 us
    pallas_call x1, Pallas kernels: 200 us -> 191 us  [run_forward(): pl.pallas_call(functools.partial(forward_kernel, dims), out_shape=[jax.Sh...]
where the time goes in v1:
time: 424 us
  Pallas kernels  420 us (99%)
    pallas_call x1, Pallas kernels, run_backward(): pl.pallas_call(functools.partial(backward_kernel, dims), out_shape=[jax.S...  216 us
    pallas_call x1, Pallas kernels, run_forward(): pl.pallas_call(functools.partial(forward_kernel, dims), out_shape=[jax.Sh...  191 us
    pallas_call x1, Pallas kernels, run_adam(): pl.pallas_call(functools.partial(adam_kernel, dims), grid=(layers, parts)...  12.1 us

profile of v1, /device:TPU:0, one launch (start us, length us, event | category | flops | bytes accessed | tf_op | source)
XLA Modules:
  0.0 423.8 jit_solution(16271137961618847986)
XLA Ops:
  1.3 0.7 convert_element_type.6
  2.0 0.6 pad_convert_fusion.refs_2_
  2.6 191.4 %forward_layers.1 = (f32[256,1024]{1,0:T(8,128)}, f32[8,1024]{1,0:T(8,128)}, bf16[2,4,2,128,3072]{4,3,2,1,0:T(8,128)(2,1)}, bf16[2,1024,1024]{2,1,0:T(8,128)(2,1...) custom-call(s32[1]{0:T(128)S(6)} %copy.46.refs_0_, ...), custom_call_target="tpu_custom_call" | custom-call | tf_op jit(solution)/shard_map/forward_layers/pallas_call | solution.py:669
  194.0 216.3 %backward_layers.1 = (f32[256,1024]{1,0:T(8,128)}, f32[8,1024]{1,0:T(8,128)}, f32[8,128]{1,0:T(8,128)}, f32[2,128,3072]{2,1,0:T(8,128)}) custom-call(s32[1]{0:T(128)S(6)} %copy.46.refs_0_, bf16[256,1024]{1,0:T(8,128)(2,1)} %bitcast.18, f32[8,1024]{1,0:T(8,128)} %get-tuple-element.71.refs_2_, bf16[2,4,2,128,3072]{4,3,2,1,0:T(8,128)(2,1)} %get-tuple-element.72.refs_3_, ...), custom_call_target="tpu_custom_call" | custom-call | tf_op jit(solution)/shard_map/backward_layers/pallas_call | solution.py:1098
  410.3 1.2 slice.3
  411.5 12.1 %adam_update.1 = (f32[256,1024]{1,0:T(8,128)}, f32[256,1024]{1,0:T(8,128)}, f32[2,3,128,256]{3,2,1,0:T(8,128)}, f32[2,256,128]{2,1,0:T(8,128)}, f32[2,128,1024]{...) custom-call(f32[8,128]{1,0:T(8,128)} %get-tuple-element.82.refs_0_, ...), custom_call_target="tpu_custom_call" | custom-call | tf_op jit(solution)/shard_map/adam_update/pallas_call | solution.py:1245

commit v2 on v1

--- a/solution.py
+++ b/solution.py
@@ -33,8 +33,8 @@
     ((5, 6), (20, 21)),
     ((7,), (22,)),
     ((8,), (23,)),
-    ((9,), ()),
-    ((10, 11), ()),
+    ((9, 10), ()),
+    ((11,), ()),
     ((12, 13, 14, 15), ()),
 )
 
@@ -337,16 +337,17 @@
         del refs[:count]
         return out
 
-    lengths, x_in, norm_in = take(3)
+    lengths, x_in, g_in, norm_in = take(4)
     masters = take(4)
     out, norm_out = take(2)
-    w_save = take(1)[0]
+    g_save, w_save = take(2)
     xn1_save, xn2_save, qkv_save, ctx_save, lse_save, act_save, dact_save, hid_save, mid_save = take(9)
     w = take(1)[0]
     xn1, xn2, qkv, ctx, lse, act, dact, hid, mid, upper, norm_place, bias, turned = take(13)
     sbuf, rbuf, ysend, yrecv, acc, nslots = take(6)
     zsend, zrecv, xsend, xrecv, wsave_sem = take(5)
     ag_send, ag_recv, rs_send, rs_recv, ns_send, ns_recv, save_sem = take(7)
+    g_low, g_sem = take(2)
 
     p = Place(zn, xn, yn)
     z_order = near_first(zn)
@@ -461,6 +462,19 @@
     for u in range(ahead(-1)):
         prepare(u)
         start_unit(u)
+    first = p.seq * block
+    g_zero = Gather(p, g_save, block, ag_send.at[2 * layers], ag_recv.at[2 * layers])
+
+    def mask_in(i, unused):
+        at = rows_of(i, 32)
+        slot = first + i * 32 + lax.broadcasted_iota(jnp.int32, (32, 1), 0)
+        g_low[at, :] = jnp.where(slot < length, g_in[at, :].astype(F32), 0.0).astype(BF16)
+        return unused
+
+    lax.fori_loop(0, block // 32, mask_in, 0)
+    g_own = pltpu.make_async_copy(g_low, g_save.at[rows_of(p.seq, block)], g_sem.at[0])
+    g_own.start()
+    g_own.wait()
     piece = width // (groups * CORES * yn)
     at_lane = (p.dp * CORES * yn + p.seq) * piece
     norm_place[...] = jnp.zeros_like(norm_place)
@@ -473,7 +487,6 @@
         hid[0, at, :] = x_in[at, :].astype(F32)
 
     row_loop(block, 64, load_in)
-    first = p.seq * block
 
     def norm_row(index):
         return norm_out[pl.ds(index, 1), :]
@@ -549,6 +562,11 @@
 
         g_one.wait_chip()
         g_one.forward()
+
+        @pl.when(l == 0)
+        def _():
+            g_zero.start()
+
         need(l, 0, 3)
         project(p.seq_at(0, 0))
         project(p.seq_at(0, 1))
@@ -566,6 +584,12 @@
         need(l, 3, 4)
         rs[0].start(lambda b: mm_nt(ctx[l, rows_of(b, block), :], weight(l, cols_o)))
         pumps(l, *PUMPS[3])
+
+        @pl.when(l == 0)
+        def _():
+            g_zero.wait_chip()
+            g_zero.forward()
+
         rs[0].wait()
 
         def add_middle(at):
@@ -639,10 +663,11 @@
             item.wait()
         return unused
 
+    g_zero.wait_rest()
     lax.fori_loop(0, layers, finish, 0)
 
 
-def run_forward(dims, lengths, x_in, norm_in, masters):
+def run_forward(dims, lengths, x_in, g_in, norm_in, masters):
     (layers, slots, width, block, local_width, local_ff, groups, zn, xn, yn) = dims
     shard = width // groups
     slot_count, sem_count = sum_slots(zn, xn, yn)
@@ -672,9 +697,10 @@
             jax.ShapeDtypeStruct((block, width), F32),
             jax.ShapeDtypeStruct((4 * layers, width), F32),
         ]
+        + [jax.ShapeDtypeStruct((slots, width), BF16)]
         + kept,
-        in_specs=[smem] + [vmem] * 6,
-        out_specs=[vmem, vmem] + [hbm] * len(kept),
+        in_specs=[smem] + [vmem] * 7,
+        out_specs=[vmem, vmem] + [hbm] * (1 + len(kept)),
         scratch_shapes=[pltpu.VMEM(k.shape, k.dtype) for k in kept]
         + [
             pltpu.VMEM((block, local_ff), F32),
@@ -692,19 +718,21 @@
             dma((UNITS * layers, xn - 1, zn)),
             dma((UNITS * layers, xn - 1, zn)),
             dma((layers,)),
-            dma((2 * layers, 2 * yn - 1)),
-            dma((2 * layers, 2 * yn - 1)),
+            dma((2 * layers + 1, 2 * yn - 1)),
+            dma((2 * layers + 1, 2 * yn - 1)),
             dma((2 * layers, 2 * yn - 1)),
             dma((2 * layers, 2 * yn - 1)),
             dma((sem_count,)),
             dma((sem_count,)),
             dma((layers, 9)),
+            pltpu.VMEM((block, width), BF16),
+            dma((1,)),
         ],
         compiler_params=pltpu.CompilerParams(
             collective_id=0, has_side_effects=True, vmem_limit_bytes=62 * 2**20
         ),
         name="forward_layers",
-    )(lengths, x_in, norm_in, *masters)
+    )(lengths, x_in, g_in, norm_in, *masters)
 
 def backward_kernel(dims, *refs):
     (layers, slots, width, block, local_width, local_ff, groups, zn, xn, yn) = dims
@@ -718,7 +746,7 @@
         del refs[:count]
         return out
 
-    lengths, g_in, norms = take(3)
+    lengths, g_in, norms, g_all = take(4)
     kept = take(10)
     g_out, norm_grad, total_out = take(3)
     shards = take(1)[0]
@@ -929,8 +957,6 @@
     def layer(step, unused):
         l = layers - 1 - step
         later = l + 1
-        for which in load_order:
-            load(l, which).start()
         g_one = Gather(p, gfull, block, ag_send.at[2 * l], ag_recv.at[2 * l])
         g_two = Gather(p, gbfull, block, ag_send.at[2 * l + 1], ag_recv.at[2 * l + 1])
         rs = [
@@ -945,11 +971,26 @@
             gfull[at, :] = g[rows_of(i, 32), :].astype(BF16)
             return unused
 
-        lax.fori_loop(0, block // 32, low_in, 0)
-        g_one.start()
-
+        all_in = pltpu.make_async_copy(g_all, gfull, load_sem.at[13])
+
+        @pl.when(step == 0)
+        def _():
+            all_in.start()
+
+        @pl.when(step > 0)
+        def _():
+            lax.fori_loop(0, block // 32, low_in, 0)
+            g_one.start()
+
+        for which in load_order:
+            load(l, which).start()
         load(l, 3).wait()
         load(l, 10).wait()
+
+        @pl.when(step == 0)
+        def _():
+            all_in.wait()
+
 
         def upper_grad(index):
             at = rows_of(index, block)
@@ -957,16 +998,23 @@
             gu[at, :] = (value * dact[at, :].astype(F32)).astype(BF16)
 
         upper_grad(p.seq_at(0, 0))
-        g_one.wait_chip()
+
+        @pl.when(step > 0)
+        def _():
+            g_one.wait_chip()
+
         upper_grad(p.seq_at(0, 1))
-        g_one.forward()
+
+        @pl.when(step > 0)
+        def _():
+            g_one.forward()
 
         @pl.when(step > 0)
         def _():
             reduce_x(later, 0)
             send_x(later, 2)
-
-        g_one.wait_rest()
+            g_one.wait_rest()
+
         for k in range(1, yn):
             upper_grad(p.seq_at(-k, 0))
             upper_grad(p.seq_at(-k, 1))
@@ -1086,7 +1134,7 @@
     total_out[...] = jnp.broadcast_to(jnp.sqrt(total), (8, 128))
 
 
-def run_backward(dims, lengths, g_in, norms, kept):
+def run_backward(dims, lengths, g_in, norms, g_all, kept):
     (layers, slots, width, block, local_width, local_ff, groups, zn, xn, yn) = dims
     packed = UNITS * local_width
     shard = width // groups
@@ -1103,7 +1151,7 @@
             jax.ShapeDtypeStruct((8, 128), F32),
             jax.ShapeDtypeStruct((layers, shard, packed), F32),
         ],
-        in_specs=[smem, vmem, vmem] + [hbm] * len(kept),
+        in_specs=[smem, vmem, vmem] + [hbm] * (1 + len(kept)),
         out_specs=[vmem] * 4,
         scratch_shapes=[pltpu.VMEM(k.shape[1:], k.dtype) for k in kept]
         + [
@@ -1140,13 +1188,13 @@
             dma((sem_count,)),
             dma((CORES * yn + groups - 2,)),
             dma((CORES * yn + groups - 2,)),
-            dma((len(kept) + 3,)),
+            dma((len(kept) + 4,)),
         ],
         compiler_params=pltpu.CompilerParams(
             collective_id=1, has_side_effects=True, vmem_limit_bytes=62 * 2**20
         ),
         name="backward_layers",
-    )(lengths, g_in, norms, *kept)
+    )(lengths, g_in, norms, g_all, *kept)
 
 
 def adam_kernel(dims, *refs):
@@ -1295,8 +1343,9 @@
     norm_in = norm_params.astype(BF16).astype(F32).reshape(4 * layer_count, piece)
     norm_in = jnp.pad(norm_in, ((0, 0), (0, 128 - piece)))
     flat = (local_slots, width)
-    kept = run_forward(dims, row_lengths, block_input.reshape(flat), norm_in, masters[:4])
-    back = run_backward(dims, row_lengths, output_grad.reshape(flat), kept[1], kept[2:])
+    g_in = output_grad.reshape(flat)
+    kept = run_forward(dims, row_lengths, block_input.reshape(flat), g_in, norm_in, masters[:4])
+    back = run_backward(dims, row_lengths, g_in, kept[1], kept[2], kept[3:])
     outs = run_adam(dims, back[2], back[1], kept[0], back[0], back[3], masters, firsts, seconds)
     whole = (row_count,) + flat
     final = [outs[0].reshape(whole), outs[1].reshape(whole), back[2][0, 0]]

time: 424 us -> 412 us (0.972)
  Pallas kernels: 420 us -> 408 us
    pallas_call x1, Pallas kernels: 216 us -> 204 us  [run_backward(): pl.pallas_call(functools.partial(backward_kernel, dims), out_shape=[jax.S...]
where the time goes in v2:
time: 412 us
  Pallas kernels  408 us (99%)
    pallas_call x1, Pallas kernels, run_backward(): pl.pallas_call(functools.partial(backward_kernel, dims), out_shape=[jax.S...  204 us
    pallas_call x1, Pallas kernels, run_forward(): pl.pallas_call(functools.partial(forward_kernel, dims), out_shape=[jax.Sh...  191 us
    pallas_call x1, Pallas kernels, run_adam(): pl.pallas_call(functools.partial(adam_kernel, dims), grid=(layers, parts)...  12.1 us

profile of v2, /device:TPU:0, one launch (start us, length us, event | category | flops | bytes accessed | tf_op | source)
XLA Modules:
  0.0 411.8 jit_solution(16845744661812930758)
XLA Ops:
  1.3 0.7 convert_element_type.6
  2.0 0.6 pad_convert_fusion.refs_3_
  2.6 191.5 %forward_layers.1 = (f32[256,1024]{1,0:T(8,128)}, f32[8,1024]{1,0:T(8,128)}, bf16[1024,1024]{1,0:T(8,128)(2,1)}, bf16[2,4,2,128,3072]{4,3,2,1,0:T(8,128)(2,1)}, ...) custom-call(s32[1]{0:T(128)S(6)} %copy.46.refs_0_, ...), custom_call_target="tpu_custom_call" | custom-call | tf_op jit(solution)/shard_map/forward_layers/pallas_call | solution.py:694
  194.1 204.2 %backward_layers.1 = (f32[256,1024]{1,0:T(8,128)}, f32[8,1024]{1,0:T(8,128)}, f32[8,128]{1,0:T(8,128)}, f32[2,128,3072]{2,1,0:T(8,128)}) custom-call(s32[1]{0:T(128)S(6)} %copy.46.refs_0_, bf16[256,1024]{1,0:T(8,128)(2,1)} %bitcast.17, f32[8,1024]{1,0:T(8,128)} %get-tuple-element.72.refs_2_, bf16[1024,1024]{1,0:T(8,128)(2,1)} %get-tuple-element.73.refs_3_, ...), custom_call_target="tpu_custom_call" | custom-call | tf_op jit(solution)/shard_map/backward_layers/pallas_call | solution.py:1146
  398.4 1.2 slice.3
  399.6 12.1 %adam_update.1 = (f32[256,1024]{1,0:T(8,128)}, f32[256,1024]{1,0:T(8,128)}, f32[2,3,128,256]{3,2,1,0:T(8,128)}, f32[2,256,128]{2,1,0:T(8,128)}, f32[2,128,1024]{...) custom-call(f32[8,128]{1,0:T(8,128)} %get-tuple-element.84.refs_0_, ...), custom_call_target="tpu_custom_call" | custom-call | tf_op jit(solution)/shard_map/adam_update/pallas_call | solution.py:1293

commit v3 on v2

--- a/solution.py
+++ b/solution.py
@@ -1111,9 +1111,6 @@
     reduce_x(0, 1, 2)
     g_out[...] = g[...]
     norm_grad[...] = all_sum(p, npart[...], nslots, ns_send, ns_recv)
-    reduce_z(0, 3, 12)
-    reduce_z(0, 0, 3)
-
     def squares(i, total):
         l, at = i // (shard // 8), rows_of(lax.rem(i, shard // 8), 8)
         value = shards[l, at, :]
@@ -1122,7 +1119,11 @@
             total = total + value[:, c * 128 : (c + 1) * 128]
         return total
 
-    tile = lax.fori_loop(0, layers * shard // 8, squares, jnp.zeros((8, 128), F32))
+    tile = jnp.zeros((8, 128), F32)
+    tile = lax.fori_loop(shard // 8, layers * shard // 8, squares, tile)
+    reduce_z(0, 3, 12)
+    reduce_z(0, 0, 3)
+    tile = lax.fori_loop(0, shard // 8, squares, tile)
     tile = all_sum_wide(p, tile, tslots, ts_send, ts_recv)
     value = norm_grad[...]
     value = value * value

time: 412 us -> 412 us (level)
  no operation moved by 1% of the time
where the time goes in v3:
time: 412 us
  Pallas kernels  408 us (99%)
    pallas_call x1, Pallas kernels, run_backward(): pl.pallas_call(functools.partial(backward_kernel, dims), out_shape=[jax.S...  204 us
    pallas_call x1, Pallas kernels, run_forward(): pl.pallas_call(functools.partial(forward_kernel, dims), out_shape=[jax.Sh...  191 us
    pallas_call x1, Pallas kernels, run_adam(): pl.pallas_call(functools.partial(adam_kernel, dims), grid=(layers, parts)...  12.1 us

profile of v3, /device:TPU:0, one launch (start us, length us, event | category | flops | bytes accessed | tf_op | source)
XLA Modules:
  0.0 411.8 jit_solution(4769039729816596628)
XLA Ops:
  1.3 0.7 convert_element_type.6
  2.0 0.6 pad_convert_fusion.refs_3_
  2.6 191.5 %forward_layers.1 = (f32[256,1024]{1,0:T(8,128)}, f32[8,1024]{1,0:T(8,128)}, bf16[1024,1024]{1,0:T(8,128)(2,1)}, bf16[2,4,2,128,3072]{4,3,2,1,0:T(8,128)(2,1)}, ...) custom-call(s32[1]{0:T(128)S(6)} %copy.46.refs_0_, ...), custom_call_target="tpu_custom_call" | custom-call | tf_op jit(solution)/shard_map/forward_layers/pallas_call | solution.py:694
  194.1 204.3 %backward_layers.1 = (f32[256,1024]{1,0:T(8,128)}, f32[8,1024]{1,0:T(8,128)}, f32[8,128]{1,0:T(8,128)}, f32[2,128,3072]{2,1,0:T(8,128)}) custom-call(s32[1]{0:T(128)S(6)} %copy.46.refs_0_, bf16[256,1024]{1,0:T(8,128)(2,1)} %bitcast.17, f32[8,1024]{1,0:T(8,128)} %get-tuple-element.72.refs_2_, bf16[1024,1024]{1,0:T(8,128)(2,1)} %get-tuple-element.73.refs_3_, ...), custom_call_target="tpu_custom_call" | custom-call | tf_op jit(solution)/shard_map/backward_layers/pallas_call | solution.py:1147
  398.4 1.2 slice.3
  399.6 12.1 %adam_update.1 = (f32[256,1024]{1,0:T(8,128)}, f32[256,1024]{1,0:T(8,128)}, f32[2,3,128,256]{3,2,1,0:T(8,128)}, f32[2,256,128]{2,1,0:T(8,128)}, f32[2,128,1024]{...) custom-call(f32[8,128]{1,0:T(8,128)} %get-tuple-element.84.refs_0_, ...), custom_call_target="tpu_custom_call" | custom-call | tf_op jit(solution)/shard_map/adam_update/pallas_call | solution.py:1294
